TPU v7x, 256 devices: a whole 4x4x8 slice. The times are simulated.
256 devices in a mesh: date: 8 (over y, core), tile: 32 (over z, x).
Axes of the slice: x: 4, y: 4, z: 8, core: 2. Of those that a mesh axis runs over, the one named last changes fastest.
Arguments:
- granules: bfloat16 [32, 10, 2560, 512], P('date', None, 'tile'), may hold values from -6 to 6
- coef_x: bfloat16 [32, 5, 128, 12], P('tile'), may hold values from -1.75 to 1.75
- coef_y: bfloat16 [32, 5, 16, 12], P('tile'), may hold values from -1.75 to 1.75
- row_offset: int32 [32, 5], P('tile'), may hold values from 0 to 36
- col_offset: int32 [32, 5], P('tile'), may hold values from 0 to 244
- targets: int32 [32, 5], P('tile'), may hold values from -1 to 31, as said below
- mask: int32 [32, 32], P(None, 'tile'), may hold values from 0 to 1, as said below
- smoother: float32 [32, 32], replicated, as said below
Outputs:
- smoothed: float32 [32, 10, 32, 2048], P(None, None, 'tile', 'date')
Inputs may be any that keep to these rules, and one draw needn't show every extreme that they name: `targets`: slot 0 of granule g names tile g; the other slots name, in an order drawn from the seed, each tile other than g within 2 of g in index once, and -1 where such a tile lies beyond the ends. `mask`: every tile has at least one valid date. `smoother`: every entry is positive.
All inputs are finite; a program needn't handle non-finite values.
Results may differ from a plain program's by a relative error of at most 0.0004.
Values sent between devices are 32-bit elements; how exact they have to be, the bound alone decides.
No kernel may reach another device: no remote copies, remote signals or barrier semaphores. Data moves between devices by JAX's collectives and lax.ppermute only.
A program may use at most 128 MiB of HBM per device.

v0:
```python
import jax
import jax.numpy as jnp
from jax import lax
from jax.sharding import PartitionSpec as P

RADIUS = 2


def shifted(block, axis, distance):
    devices = range(lax.axis_size(axis))
    route = [(i - distance, i) for i in devices if i - distance in devices]
    return lax.ppermute(block, axis, route)


def band_matrix(coeffs, offset, span_width):
    row_count = coeffs.shape[0]
    row_ids = jnp.arange(row_count, dtype=jnp.int32)[:, None]
    col_ids = jnp.arange(span_width, dtype=jnp.int32)[None, :]
    tap_index = col_ids - 2 * row_ids - offset
    banded = jnp.zeros((row_count, span_width), jnp.float32)
    for tap_number in range(coeffs.shape[1]):
        picked = coeffs[:, tap_number : tap_number + 1].astype(jnp.float32)
        banded = banded + jnp.where(tap_index == tap_number, picked, jnp.float32(0.0))
    return banded


def body(granules, coef_x, coef_y, row_offset, col_offset, targets, mask, smoother):
    local_dates, band_count, grid_rows, grid_cols = granules.shape
    slot_count = coef_x.shape[1]
    tile_cols = coef_x.shape[2]
    tile_rows = coef_y.shape[2]
    x_mats = jnp.concatenate(
        [
            band_matrix(coef_x[0, slot], col_offset[0, slot], grid_cols)
            for slot in range(slot_count)
        ],
        0,
    ).astype(jnp.bfloat16)
    x_pass = jnp.dot(granules.reshape(-1, grid_cols), x_mats.T, preferred_element_type=jnp.float32)
    x_pass = x_pass.reshape(local_dates, band_count, grid_rows, slot_count, tile_cols)
    y_mats = jnp.stack(
        [
            band_matrix(coef_y[0, slot], row_offset[0, slot], grid_rows)
            for slot in range(slot_count)
        ],
        0,
    )
    partials = jnp.einsum("kir,dbrkj->kdbij", y_mats, x_pass, precision=lax.Precision.HIGHEST)
    flat_parts = partials.reshape(slot_count, -1)
    aimed = targets[0]
    own_tile = lax.axis_index("tile")

    def aimed_at(reach):
        chosen = (aimed == own_tile + reach).astype(jnp.float32)
        return jnp.dot(chosen, flat_parts, precision=lax.Precision.HIGHEST)

    tiled = aimed_at(0)
    for reach in [step for step in range(-RADIUS, RADIUS + 1) if step != 0]:
        tiled = tiled + shifted(aimed_at(reach), "tile", reach)
    series = tiled.reshape(local_dates, band_count, tile_rows * tile_cols)
    all_dates = smoother.shape[0]
    block_pix = tile_rows * tile_cols // lax.axis_size("date")
    weight = mask[:, 0].astype(jnp.float32)
    denominator = jnp.dot(smoother, weight, precision=lax.Precision.HIGHEST)
    gathered = lax.all_to_all(series, "date", split_axis=2, concat_axis=0, tiled=True)
    weighted = gathered * weight[:, None, None]
    numerator = jnp.einsum("ts,sbp->tbp", smoother, weighted, precision=lax.Precision.HIGHEST)
    smoothed = numerator / denominator[:, None, None]
    return smoothed.reshape(all_dates, band_count, 1, block_pix)


def solution(mesh):
    return jax.shard_map(
        body,
        mesh=mesh,
        in_specs=(
            P("date", None, "tile", None),
            P("tile", None, None, None),
            P("tile", None, None, None),
            P("tile", None),
            P("tile", None),
            P("tile", None),
            P(None, "tile"),
            P(),
        ),
        out_specs=P(None, None, "tile", "date"),
        check_vma=False,
    )
```

profile of v0, /device:TPU:128, one launch (start us, length us, event | category | flops | bytes accessed | tf_op | source)
XLA Modules:
  0.0 153.5 jit_solution(16372437884035769763)
XLA Ops:
  7.6 5.6 %convolution_bitcast_fusion = f32[3200,640]{0,1:T(8,128)} fusion(bf16[640,512]{1,0:T(8,128)(2,1)S(1)} %fusion.89, bf16[3200,512]{1,0:T(8,128)(2,1)S(1)} %bitcast.399), kind=kOutput, calls=%fused_computation.2 | convolution fusion | flops 2097152000 | bytes 12124160 | tf_op jit(solution)/shard_map/dot_general | solution.py:39
  13.3 17.5 %reshape.2577 = f32[4,10,80,5,128]{2,1,0,4,3:T(8,128)} reshape(f32[3200,640]{0,1:T(8,128)} %convolution_bitcast_fusion) | data formatting | bytes 16384000 | tf_op jit(solution)/shard_map/reshape | solution.py:40
  36.4 24.8 %fusion = f32[5,4,10,128,16]{3,4,2,1,0:T(8,128)} fusion(f32[4,10,80,5,128]{2,1,0,4,3:T(8,128)} %reshape.2577, f32[5,16,80]{2,1,0:T(8,128)S(1)} %constant_dynamic-update-slice_fusion), kind=kOutput, calls=%fused_computation | convolution fusion | flops 393216000 | bytes 9856000 | tf_op jit(solution)/shard_map/kir,dbrkj->kdbij/dot_general | solution.py:48
  61.2 4.3 %fusion.8 = f32[1,81920]{1,0:T(1,128)} fusion(f32[1,5,640,128]{3,2,1,0:T(8,128)} %bitcast.400, s32[1,5]{1,0:T(1,128)S(1)} %copy-done.5, s32[]{:T(128)S(6)} %add.849), kind=kOutput, calls=%fused_computation.9 | convolution fusion | flops 4915205 | bytes 1966104 | tf_op jit(solution)/shard_map/dot_general | solution.py:55
  65.6 4.5 %collective-permute-start = (f32[81920]{0:T(1024)}, f32[81920]{0:T(1024)}, u32[]{:S(2)}, u32[]{:S(2)}) collective-permute-start(f32[81920]{0:T(1024)} %bitcast.90), channel_id=1, source_target_pairs={{2,0},{3,1},{4,2},{5,3},{6,4},{7,5},{8,6},{9,7},{10,8},{11,9},{12,... | collective-permute-start | bytes 983048 | tf_op jit(solution)/shard_map/ppermute | solution.py:12
  70.0 4.3 %fusion.6 = f32[1,81920]{1,0:T(1,128)} fusion(f32[1,5,640,128]{3,2,1,0:T(8,128)} %bitcast.401, s32[1,5]{1,0:T(1,128)S(1)} %copy-done.5, s32[]{:T(128)S(6)} %add.851), kind=kOutput, calls=%fused_computation.7 | convolution fusion | flops 4915205 | bytes 1966104 | tf_op jit(solution)/shard_map/dot_general | solution.py:55
  74.4 3.0 %collective-permute-start.1 = (f32[81920]{0:T(1024)}, f32[81920]{0:T(1024)}, u32[]{:S(2)}, u32[]{:S(2)}) collective-permute-start(f32[81920]{0:T(1024)} %bitcast.93), channel_id=1, source_target_pairs={{1,0},{2,1},{3,2},{4,3},{5,4},{6,5},{7,6},{8,7},{9,8},{10,9},{11,1... | collective-permute-start | bytes 983048 | tf_op jit(solution)/shard_map/ppermute | solution.py:12
  77.4 4.3 %fusion.4 = f32[1,81920]{1,0:T(1,128)} fusion(f32[1,5,640,128]{3,2,1,0:T(8,128)} %bitcast.402, s32[1,5]{1,0:T(1,128)S(1)} %copy-done.5, s32[]{:T(128)S(6)} %add.853), kind=kOutput, calls=%fused_computation.5 | convolution fusion | flops 4915205 | bytes 1966104 | tf_op jit(solution)/shard_map/dot_general | solution.py:55
  81.8 2.8 %collective-permute-start.2 = (f32[81920]{0:T(1024)}, f32[81920]{0:T(1024)}, u32[]{:S(2)}, u32[]{:S(2)}) collective-permute-start(f32[81920]{0:T(1024)} %bitcast.96), channel_id=1, source_target_pairs={{0,1},{1,2},{2,3},{3,4},{4,5},{5,6},{6,7},{7,8},{8,9},{9,10},{10,1... | collective-permute-start | bytes 983048 | tf_op jit(solution)/shard_map/ppermute | solution.py:12
  84.6 3.7 %fusion.2 = f32[1,81920]{1,0:T(1,128)S(1)} fusion(f32[1,5,640,128]{3,2,1,0:T(8,128)} %bitcast.403, s32[1,5]{1,0:T(1,128)S(1)} %copy-done.5, s32[]{:T(128)S(6)} %add.855), kind=kOutput, calls=%fused_computation.3 | convolution fusion | flops 4915205 | bytes 1966104 | tf_op jit(solution)/shard_map/dot_general | solution.py:55
  88.3 3.0 %collective-permute-start.3 = (f32[81920]{0:T(1024)S(1)}, f32[81920]{0:T(1024)S(1)}, u32[]{:S(2)}, u32[]{:S(2)}) collective-permute-start(f32[81920]{0:T(1024)S(1)} %bitcast.409), channel_id=1, source_target_pairs={{0,2},{1,3},{2,4},{3,5},{4,6},{5,7},{6,8},{7,9},{8,10},{9,11},{10,... | collective-permute-start | bytes 983048 | tf_op jit(solution)/shard_map/ppermute | solution.py:12
  91.3 2.2 %fusion.10 = f32[1,81920]{1,0:T(1,128)S(1)} fusion(f32[1,5,640,128]{3,2,1,0:T(8,128)S(1)} %bitcast.404, s32[1,5]{1,0:T(1,128)S(1)} %copy-done.5, s32[]{:T(128)S(6)} %axis_index.12), kind=kOutput, calls=%fused_computation.11 | convolution fusion | flops 4915205 | bytes 1966104 | tf_op jit(solution)/shard_map/dot_general | solution.py:55
  93.5 4.2 %collective-permute-done.2 = f32[81920]{0:T(1024)} collective-permute-done((f32[81920]{0:T(1024)}, f32[81920]{0:T(1024)}, u32[]{:S(2)}, u32[]{:S(2)}) %collective-permute-start.2) | collective-permute-done | bytes 327712 | tf_op jit(solution)/shard_map/ppermute | solution.py:12
  97.7 5.5 %collective-permute-done.3 = f32[81920]{0:T(1024)S(1)} collective-permute-done((f32[81920]{0:T(1024)S(1)}, f32[81920]{0:T(1024)S(1)}, u32[]{:S(2)}, u32[]{:S(2)}) %collective-permute-start.3) | collective-permute-done | bytes 327712 | tf_op jit(solution)/shard_map/ppermute | solution.py:12
  103.2 2.0 %add_add_fusion = f32[81920]{0:T(1024)} fusion(f32[81920]{0:T(1024)S(1)} %collective-permute-done.3, f32[81920]{0:T(1024)} %collective-permute-done.2, f32[81920]{0:T(1024)} %collective-permute-done.1, f32[81920]{0:T(1024)S(1)} %bitcast.408, f32[81920]{0:T(1024)} %collective-permute-done), kind=kLoop, calls=%fused_computation.22 | loop fusion | flops 327680 | bytes 1966080 | tf_op jit(solution)/shard_map/add | solution.py:59
  105.2 1.8 %reshape.2441 = f32[4,10,2048]{2,1,0:T(8,128)} reshape(f32[81920]{0:T(1024)} %add_add_fusion) | data formatting | bytes 655360 | tf_op jit(solution)/shard_map/reshape | solution.py:60
  107.0 4.5 %copy.22 = f32[4,10,2048]{1,0,2:T(4,128)} copy(f32[4,10,2048]{2,1,0:T(8,128)} %reshape.2441) | data formatting | bytes 655360 | tf_op jit(solution)/shard_map/reshape | solution.py:60
  111.5 7.3 %reshape.2638 = f32[8,1,10240]{2,1,0:T(1,128)} reshape(f32[2048,4,10]{2,1,0:T(4,128)} %bitcast.405) | data formatting | bytes 655360
  118.8 4.5 %all-to-all-start = ((f32[8,1,10240]{2,1,0:T(1,128)}), f32[8,1,10240]{2,1,0:T(1,128)}, u32[]{:S(2)}, u32[]{:S(2)}) async-start(f32[8,1,10240]{2,1,0:T(1,128)} %reshape.2638), calls=%async_computation | async-start | bytes 655360 | tf_op jit(solution)/shard_map/all_to_all | solution.py:65
  123.4 8.2 %all-to-all-done = f32[8,1,10240]{2,1,0:T(1,128)} async-done(((f32[8,1,10240]{2,1,0:T(1,128)}), f32[8,1,10240]{2,1,0:T(1,128)}, u32[]{:S(2)}, u32[]{:S(2)}) %all-to-all-start) | async-done | bytes 327712 | tf_op jit(solution)/shard_map/all_to_all | solution.py:65
  132.2 3.2 %reduce.120 = f32[8,10240]{1,0:T(8,128)} reduce(f32[8,1,10240]{2,1,0:T(1,128)} %all-to-all-done, f32[]{:T(128)} %broadcast.2156), dimensions={1}, to_apply=%all_to_all.13.reduce_sub_computation | reduce | bytes 655364 | tf_op jit(solution)/shard_map/all_to_all | solution.py:65
  135.3 8.5 %reshape.2639 = f32[2048,4,10]{2,1,0:T(4,128)} reshape(f32[8,10240]{1,0:T(8,128)} %reduce.120) | data formatting | bytes 655360
  143.9 3.5 %copy.29 = f32[4,10,8,256]{3,2,0,1:T(8,128)} copy(f32[4,10,8,256]{1,0,3,2:T(4,128)} %bitcast.406) | data formatting | bytes 655360 | tf_op jit(solution)/shard_map/all_to_all | solution.py:65
  147.4 1.8 %copy.24 = f32[8,4,10,256]{3,1,0,2:T(4,128)} copy(f32[8,4,10,256]{3,0,1,2:T(8,128)} %bitcast.407) | data formatting | bytes 655360 | tf_op jit(solution)/shard_map/all_to_all | solution.py:65
  (48 shorter events, 18.2 us)
Async XLA Ops:
  0.0 7.6 %copy-start = (bf16[4,10,80,512]{3,2,1,0:T(8,128)(2,1)S(1)}, bf16[4,10,80,512]{3,2,1,0:T(8,128)(2,1)}, u32[]{:S(2)}) copy-start(bf16[4,10,80,512]{3,2,1,0:T(8,128)(2,1)} %param.8) | copy-start | bytes 9830404
  13.3 17.5 %copy-start.2 = (bf16[1,5,16,12]{3,2,1,0:T(8,128)(2,1)S(1)}, bf16[1,5,16,12]{3,2,1,0:T(8,128)(2,1)}, u32[]{:S(2)}) copy-start(bf16[1,5,16,12]{3,2,1,0:T(8,128)(2,1)} %param.10) | copy-start | bytes 5764
  13.3 17.8 %copy-start.4 = (s32[1,5]{1,0:T(1,128)S(1)}, s32[1,5]{1,0:T(1,128)}, u32[]{:S(2)}) copy-start(s32[1,5]{1,0:T(1,128)} %param.11) | copy-start | bytes 64
  36.4 24.8 %copy-start.5 = (s32[1,5]{1,0:T(1,128)S(1)}, s32[1,5]{1,0:T(1,128)}, u32[]{:S(2)}) copy-start(s32[1,5]{1,0:T(1,128)} %param.13) | copy-start | bytes 64
  65.6 27.9 %collective-permute-start = (f32[81920]{0:T(1024)}, f32[81920]{0:T(1024)}, u32[]{:S(2)}, u32[]{:S(2)}) collective-permute-start(f32[81920]{0:T(1024)} %bitcast.90), channel_id=1, source_target_pairs={{2,0},{3,1},{4,2},{5,3},{6,4},{7,5},{8,6},{9,7},{10,8},{11,9},{12,... | collective-permute-start | bytes 983048 | tf_op jit(solution)/shard_map/ppermute | solution.py:12
  74.4 19.1 %collective-permute-start.1 = (f32[81920]{0:T(1024)}, f32[81920]{0:T(1024)}, u32[]{:S(2)}, u32[]{:S(2)}) collective-permute-start(f32[81920]{0:T(1024)} %bitcast.93), channel_id=1, source_target_pairs={{1,0},{2,1},{3,2},{4,3},{5,4},{6,5},{7,6},{8,7},{9,8},{10,9},{11,1... | collective-permute-start | bytes 983048 | tf_op jit(solution)/shard_map/ppermute | solution.py:12
  81.8 15.9 %collective-permute-start.2 = (f32[81920]{0:T(1024)}, f32[81920]{0:T(1024)}, u32[]{:S(2)}, u32[]{:S(2)}) collective-permute-start(f32[81920]{0:T(1024)} %bitcast.96), channel_id=1, source_target_pairs={{0,1},{1,2},{2,3},{3,4},{4,5},{5,6},{6,7},{7,8},{8,9},{9,10},{10,1... | collective-permute-start | bytes 983048 | tf_op jit(solution)/shard_map/ppermute | solution.py:12
  84.6 6.7 %copy-start.1 = (f32[5,4,10,128,16]{3,4,2,1,0:T(8,128)S(1)}, f32[5,4,10,128,16]{3,4,2,1,0:T(8,128)}, u32[]{:S(2)}) copy-start(f32[5,4,10,128,16]{3,4,2,1,0:T(8,128)} %fusion) | copy-start | bytes 4915204
  88.3 14.9 %collective-permute-start.3 = (f32[81920]{0:T(1024)S(1)}, f32[81920]{0:T(1024)S(1)}, u32[]{:S(2)}, u32[]{:S(2)}) collective-permute-start(f32[81920]{0:T(1024)S(1)} %bitcast.409), channel_id=1, source_target_pairs={{0,2},{1,3},{2,4},{3,5},{4,6},{5,7},{6,8},{7,9},{8,10},{9,11},{10,... | collective-permute-start | bytes 983048 | tf_op jit(solution)/shard_map/ppermute | solution.py:12
  111.5 11.7 %copy-start.3 = (f32[32,32]{1,0:T(8,128)S(1)}, f32[32,32]{1,0:T(8,128)}, u32[]{:S(2)}) copy-start(f32[32,32]{1,0:T(8,128)} %param.15) | copy-start | bytes 12292
  111.5 11.7 %copy-start.6 = (s32[32,1]{0,1:T(1,128)S(1)}, s32[32,1]{0,1:T(1,128)}, u32[]{:S(2)}) copy-start(s32[32,1]{0,1:T(1,128)} %param.14) | copy-start | bytes 388
  118.8 12.8 %all-to-all-start = ((f32[8,1,10240]{2,1,0:T(1,128)}), f32[8,1,10240]{2,1,0:T(1,128)}, u32[]{:S(2)}, u32[]{:S(2)}) async-start(f32[8,1,10240]{2,1,0:T(1,128)} %reshape.2638), calls=%async_computation | async-start | bytes 655360 | tf_op jit(solution)/shard_map/all_to_all | solution.py:65
where the time goes:
time: 155 us; the launch traced here: 154 us
  local copies, waits for them, and re-layouts  51.5 us (33%)
  matrix products  51 us (33%)
  waiting for transfers between devices  17.9 us (12%)
  starting transfers between devices  17.7 us (11%)
  other arithmetic  15.2 us (10%)
    dot_general x1, matrix products, body(): jnp.einsum('kir,dbrkj->kdbij', y_mats, x_pass, precision=lax.Precision.HI...  24.8 us
    dot_general x5, matrix products, aimed_at(): return jnp.dot(chosen, flat_parts, precision=lax.Precision.HIGHEST)  19 us
    reshape x1, local copies, waits for them, and re-layouts, body(): x_pass.reshape(local_dates, band_count, grid_rows, slot_count, tile_cols)  17.5 us
    unnamed x16, local copies, waits for them, and re-layouts  15.8 us
    ppermute x4, starting transfers between devices, shifted(): return lax.ppermute(block, axis, route)  13.2 us
    ppermute x4, waiting for transfers between devices, shifted(): return lax.ppermute(block, axis, route)  9.67 us
    all_to_all x1, waiting for transfers between devices, body(): lax.all_to_all(series, 'date', split_axis=2, concat_axis=0, tiled=True)  8.2 us
    all_to_all x4, local copies, waits for them, and re-layouts, body(): lax.all_to_all(series, 'date', split_axis=2, concat_axis=0, tiled=True)  7.72 us
  transfers between devices with their start and end apart: 5, of which 3 were waited for; matrix products, arithmetic and copies ran while one was open for 10% of the time, Pallas kernels for 0%

commit v1 on v0

v1 whole, which is shorter than its diff:
```python
import functools

import jax
import jax.numpy as jnp
from jax import lax
from jax.experimental import pallas as pl
from jax.experimental.pallas import tpu as pltpu
from jax.sharding import PartitionSpec as P

HIGHEST = lax.Precision.HIGHEST


def even_swap(block):
    pairs = [(i, i ^ 1) for i in range(lax.axis_size("tile"))]
    return lax.ppermute(block, "tile", pairs)


def odd_swap(block):
    last = lax.axis_size("tile") - 1
    pairs = [(i, i if i in (0, last) else ((i - 1) ^ 1) + 1) for i in range(last + 1)]
    return lax.ppermute(block, "tile", pairs)


def resample_kernel(reaches, targets, row_offset, col_offset, coef_x, coef_y, granule, *rest):
    count = len(reaches)
    outs, (x_mats, y_mats) = rest[:count], rest[count:]
    slots = coef_x.shape[1]
    tile_cols, taps = coef_x.shape[2:]
    tile_rows = coef_y.shape[2]
    bands, grid_rows, grid_cols = granule.shape[1:]
    date = pl.program_id(0)

    @pl.when(date == 0)
    def build():
        own = lax.axis_index("tile")
        side = 1 - 2 * lax.rem(own, 2)
        to_order = (
            lax.broadcasted_iota(jnp.int32, (tile_rows, tile_rows), 1)
            == 2 * lax.rem(lax.broadcasted_iota(jnp.int32, (tile_rows, tile_rows), 0), tile_rows // 2)
            + lax.broadcasted_iota(jnp.int32, (tile_rows, tile_rows), 0) // (tile_rows // 2)
        ).astype(jnp.float32)
        for n, reach in enumerate(reaches):
            wanted = own + side * reach
            slot = jnp.int32(0)
            used = jnp.int32(0)
            for k in range(slots):
                hit = jnp.logical_and(wanted >= 0, targets[0, k] == wanted).astype(jnp.int32)
                slot = slot + k * hit
                used = used + hit
            tap = (
                lax.broadcasted_iota(jnp.int32, (tile_cols, grid_cols), 1)
                - 2 * lax.broadcasted_iota(jnp.int32, (tile_cols, grid_cols), 0)
                - col_offset[0, slot]
            )
            coeffs = coef_x[0, slot].astype(jnp.float32)
            banded = jnp.zeros((tile_cols, grid_cols), jnp.float32)
            for t in range(taps):
                banded = jnp.where(tap == t, coeffs[:, t : t + 1], banded)
            x_mats[n] = banded.astype(jnp.bfloat16)
            tap = (
                lax.broadcasted_iota(jnp.int32, (tile_rows, grid_rows), 1)
                - 2 * lax.broadcasted_iota(jnp.int32, (tile_rows, grid_rows), 0)
                - row_offset[0, slot]
            )
            tap = jnp.where(used > 0, tap, -1)
            coeffs = coef_y[0, slot].astype(jnp.float32)
            banded = jnp.zeros((tile_rows, grid_rows), jnp.float32)
            for t in range(taps):
                banded = jnp.where(tap == t, coeffs[:, t : t + 1], banded)
            ordered = jnp.dot(to_order, banded, preferred_element_type=jnp.float32)
            y_mats[n * tile_rows : (n + 1) * tile_rows] = ordered.astype(jnp.bfloat16)

    along_y = [
        jnp.dot(y_mats[...], granule[0, b], preferred_element_type=jnp.float32) for b in range(bands)
    ]
    half = tile_rows // 2
    for n in range(count):
        rows = jnp.concatenate([part[n * tile_rows : (n + 1) * tile_rows] for part in along_y], 0)
        high = rows.astype(jnp.bfloat16)
        low = (rows - high.astype(jnp.float32)).astype(jnp.bfloat16)
        both = lax.dot_general(
            jnp.concatenate([high, low], 0),
            x_mats[n],
            (((1,), (1,)), ((), ())),
            preferred_element_type=jnp.float32,
        )
        partial = both[: bands * tile_rows] + both[bands * tile_rows :]
        stride = outs[n].shape[0] // half
        for b in range(bands):
            for parity in range(2):
                first = b * tile_rows + parity * half
                outs[n][pl.ds(date * 2 * bands + parity * bands + b, half, stride=stride), :] = partial[
                    first : first + half
                ]


def resample(reaches, chunk, chunks, targets, row_offset, col_offset, coef_x, coef_y, granules):
    dates, bands, grid_rows, grid_cols = granules.shape
    slots, tile_cols = coef_x.shape[1:3]
    tile_rows = coef_y.shape[2]
    bands = bands // chunks
    rows = dates * bands * tile_rows
    count = len(reaches)
    smem = pl.BlockSpec(memory_space=pltpu.SMEM)
    return pl.pallas_call(
        functools.partial(resample_kernel, reaches),
        grid=(dates,),
        in_specs=[
            smem,
            smem,
            smem,
            pl.BlockSpec(coef_x.shape, lambda d: (0, 0, 0, 0)),
            pl.BlockSpec(coef_y.shape, lambda d: (0, 0, 0, 0)),
            pl.BlockSpec((1, bands, grid_rows, grid_cols), lambda d: (d, chunk, 0, 0)),
        ],
        out_specs=[pl.BlockSpec((rows, tile_cols), lambda d: (0, 0))] * count,
        out_shape=[jax.ShapeDtypeStruct((rows, tile_cols), jnp.float32)] * count,
        scratch_shapes=[
            pltpu.VMEM((count, tile_cols, grid_cols), jnp.bfloat16),
            pltpu.VMEM((count * tile_rows, grid_rows), jnp.bfloat16),
        ],
        compiler_params=pltpu.CompilerParams(vmem_limit_bytes=32 * 1024 * 1024),
        cost_estimate=pl.CostEstimate(
            flops=count * dates * bands * tile_rows * grid_cols * (grid_rows + 4 * tile_cols),
            bytes_accessed=granules.size * 2 // chunks,
            transcendentals=0,
        ),
        name="resample",
    )(targets, row_offset, col_offset, coef_x, coef_y, granules)


def smooth_kernel(parts, mask, smoother, *refs):
    series, out = refs[:-1], refs[-1]
    dates = smoother.shape[0]
    lanes = out.shape[1]
    weight = jnp.broadcast_to(mask[...].astype(jnp.float32), (dates, lanes))
    weights = smoother[...]
    denominator = jnp.dot(weights, weight, precision=HIGHEST, preferred_element_type=jnp.float32)
    stride = out.shape[0] // dates
    bands = series[0].shape[0] // dates // 2
    for c in range(parts):
        for b in range(bands):
            for parity in range(2):
                picked = series[c][pl.ds(parity * bands + b, dates, stride=2 * bands), :]
                total = jnp.dot(
                    weights, picked * weight, precision=HIGHEST, preferred_element_type=jnp.float32
                )
                out[pl.ds(2 * (c * bands + b) + parity, dates, stride=stride), :] = total / denominator


def smooth(mask, smoother, series):
    rows = sum(part.shape[0] for part in series)
    lanes = series[0].shape[1]
    return pl.pallas_call(
        functools.partial(smooth_kernel, len(series)),
        out_shape=jax.ShapeDtypeStruct((rows, lanes), jnp.float32),
        compiler_params=pltpu.CompilerParams(vmem_limit_bytes=32 * 1024 * 1024),
        name="smooth",
    )(mask, smoother, *series)


def to_pixel_blocks(part):
    return lax.all_to_all(part, "date", split_axis=0, concat_axis=0, tiled=True)


CHUNKS = 1


def body(granules, coef_x, coef_y, row_offset, col_offset, targets, mask, smoother):
    bands = granules.shape[1]
    block_pix = coef_x.shape[2] * coef_y.shape[2] // lax.axis_size("date")

    def run(reaches, chunk):
        return resample(
            reaches, chunk, CHUNKS, targets, row_offset, col_offset, coef_x, coef_y, granules
        )

    far = [run((2, -2), c) for c in range(CHUNKS)]
    passed = [(even_swap(even), odd_swap(odd)) for even, odd in far]
    near = [run((1, -1, 0), c) for c in range(CHUNKS)]
    arrived = [
        (even_swap(even + from_odd), odd_swap(odd + from_even))
        for (even, odd, _), (from_even, from_odd) in zip(near, passed)
    ]
    series = [own + even + odd for (_, _, own), (even, odd) in zip(near, arrived)]
    blocks = [to_pixel_blocks(part) for part in series]
    smoothed = smooth(mask, smoother, blocks)
    return smoothed.reshape(smoother.shape[0], bands, 1, block_pix)


def solution(mesh):
    return jax.shard_map(
        body,
        mesh=mesh,
        in_specs=(
            P("date", None, "tile", None),
            P("tile", None, None, None),
            P("tile", None, None, None),
            P("tile", None),
            P("tile", None),
            P("tile", None),
            P(None, "tile"),
            P(),
        ),
        out_specs=P(None, None, "tile", "date"),
        check_vma=False,
    )
```

time: 155 us -> 52.8 us (0.34)
  matrix products: 51 us -> 0 us
  local copies, waits for them, and re-layouts: 51.5 us -> 5.62 us
  other arithmetic: 15.2 us -> 0.86 us
  Pallas kernels: 0 us -> 8.93 us
  waiting for transfers between devices: 17.9 us -> 23.3 us
  starting transfers between devices: 17.7 us -> 13.7 us
    dot_general x9 -> x0, matrix products: 51 us -> none  [the longest x1 24.8 us: body(): jnp.einsum('kir,dbrkj->kdbij', y_mats, x_pass, precision=lax.Precision.HI...]
    reshape x4 -> x0, local copies, waits for them, and re-layouts: 24.9 us -> none  [the longest x1 17.5 us: body(): x_pass.reshape(local_dates, band_count, grid_rows, slot_count, tile_cols)]
    unnamed x16, local copies, waits for them, and re-layouts: 15.8 us -> 5.62 us
    pallas_call x0 -> x3, Pallas kernels: none -> 8.93 us  [the longest x2 7.59 us: resample(): pl.pallas_call(functools.partial(resample_kernel, reaches), grid=(dates,)...]
    all_to_all x4 -> x0, local copies, waits for them, and re-layouts: 7.72 us -> none  [body(): lax.all_to_all(series, 'date', split_axis=2, concat_axis=0, tiled=True)]
    unnamed x8 -> x0, other arithmetic: 6.89 us -> none
    ppermute x4, waiting for transfers between devices: 9.67 us -> 15.1 us  [the longest x2 10.8 us: odd_swap(): return lax.ppermute(block, 'tile', pairs)]
    ppermute x4, starting transfers between devices: 13.2 us -> 9.26 us  [the longest x2 8.4 us: odd_swap(): return lax.ppermute(block, 'tile', pairs)]
  transfers between devices with their start and end apart: 5 -> 5, of which waited for: 3 -> 4; matrix products, arithmetic and copies ran while one was open for 10% -> 0% of each run, Pallas kernels for 0% -> 8%
where the time goes in v1:
time: 52.8 us; the launch traced here: 52.4 us
  waiting for transfers between devices  23.3 us (44%)
  starting transfers between devices  13.7 us (26%)
  Pallas kernels  8.93 us (17%)
  local copies, waits for them, and re-layouts  5.62 us (11%)
  other arithmetic  0.86 us (2%)
    ppermute x2, waiting for transfers between devices, odd_swap(): return lax.ppermute(block, 'tile', pairs)  10.8 us
    ppermute x2, starting transfers between devices, odd_swap(): return lax.ppermute(block, 'tile', pairs)  8.4 us
    all_to_all x1, waiting for transfers between devices, to_pixel_blocks(): return lax.all_to_all(part, 'date', split_axis=0, concat_axis=0, tiled=True)  8.15 us
    pallas_call x2, Pallas kernels, resample(): pl.pallas_call(functools.partial(resample_kernel, reaches), grid=(dates,)...  7.59 us
    unnamed x16, local copies, waits for them, and re-layouts  5.62 us
    all_to_all x1, starting transfers between devices, to_pixel_blocks(): return lax.all_to_all(part, 'date', split_axis=0, concat_axis=0, tiled=True)  4.39 us
    ppermute x2, waiting for transfers between devices, even_swap(): return lax.ppermute(block, 'tile', pairs)  4.35 us
    pallas_call x1, Pallas kernels, smooth(): pl.pallas_call(functools.partial(smooth_kernel, len(series)), out_shape=j...  1.34 us
  transfers between devices with their start and end apart: 5, of which 4 were waited for; matrix products, arithmetic and copies ran while one was open for 0% of the time, Pallas kernels for 8%

profile of v1, /device:TPU:128, one launch (start us, length us, event | category | flops | bytes accessed | tf_op | source)
XLA Modules:
  0.0 52.4 jit_solution(13836152194858622647)
XLA Ops:
  0.0 0.9 %copy.13.coef_x = bf16[1,5,128,12]{3,2,1,0:T(8,128)(2,1)S(1)} copy(bf16[1,5,128,12]{2,3,1,0:T(8,128)(2,1)} %param.9) | data formatting | bytes 30720 | tf_op args[1]
  0.9 0.0 copy-start
  0.9 1.9 %copy-done = bf16[4,10,80,512]{3,2,1,0:T(8,128)(2,1)S(1)} copy-done((bf16[4,10,80,512]{3,2,1,0:T(8,128)(2,1)S(1)}, bf16[4,10,80,512]{3,2,1,0:T(8,128)(2,1)}, u32[]{:S(2)}) %copy-start) | copy-done | bytes 3276824
  2.8 0.7 %copy-done.1 = bf16[1,5,16,12]{3,2,1,0:T(8,128)(2,1)S(1)} copy-done((bf16[1,5,16,12]{3,2,1,0:T(8,128)(2,1)S(1)}, bf16[1,5,16,12]{3,2,1,0:T(8,128)(2,1)}, u32[]{:S(2)}) %copy-start.1) | copy-done | bytes 1944
  3.6 0.7 %copy-done.3 = s32[1,5]{1,0:T(1,128)S(1)} copy-done((s32[1,5]{1,0:T(1,128)S(1)}, s32[1,5]{1,0:T(1,128)}, u32[]{:S(2)}) %copy-start.3) | copy-done | bytes 44
  4.2 0.7 %copy-done.4 = s32[1,5]{1,0:T(1,128)S(1)} copy-done((s32[1,5]{1,0:T(1,128)S(1)}, s32[1,5]{1,0:T(1,128)}, u32[]{:S(2)}) %copy-start.4) | copy-done | bytes 44
  4.9 0.7 %copy-done.5 = s32[1,5]{1,0:T(1,128)S(1)} copy-done((s32[1,5]{1,0:T(1,128)S(1)}, s32[1,5]{1,0:T(1,128)}, u32[]{:S(2)}) %copy-start.5) | copy-done | bytes 44
  5.5 3.4 %resample.3 = (f32[640,128]{1,0:T(8,128)S(1)}, f32[640,128]{1,0:T(8,128)S(1)}) custom-call(s32[1,5]{1,0:T(1,128)S(1)} %copy-done.3, s32[1,5]{1,0:T(1,128)S(1)} %copy-done.4, s32[1,5]{1,0:T(1,128)S(1)} %copy-done.5, bf16[1,5,128,12]{3,2,1,0:T(8,128)(2,1)S(1)} %copy.13.coef_x, bf16[1,5,16,12]{3,2,1,0:T(8,128)(2,1)S(1)} %copy-done.1, ...), custom_call_target="tpu_custom_call" | custom-call | flops 387973120 | bytes 3276800 | tf_op jit(solution)/shard_map/resample/pallas_call | solution.py:105
  9.0 4.2 %collective-permute-start = (f32[640,128]{1,0:T(8,128)S(1)}, f32[640,128]{1,0:T(8,128)S(1)}, u32[]{:S(2)}, u32[]{:S(2)}) collective-permute-start(f32[640,128]{1,0:T(8,128)S(1)} %get-tuple-element.12), channel_id=1, source_target_pairs={{0,0},{1,2},{2,1},{3,4},{4,3},{5,6},{6,5},{7,8},{8,7},{9,10},{10,9... | collective-permute-start | bytes 983048 | tf_op jit(solution)/shard_map/ppermute | solution.py:21
  13.2 0.0 copy-start.6
  13.2 0.0 copy-start.2
  13.2 0.8 %collective-permute-start.2 = (f32[640,128]{1,0:T(8,128)S(1)}, f32[640,128]{1,0:T(8,128)S(1)}, u32[]{:S(2)}, u32[]{:S(2)}) collective-permute-start(f32[640,128]{1,0:T(8,128)S(1)} %get-tuple-element.14), channel_id=1, source_target_pairs={{0,1},{1,0},{2,3},{3,2},{4,5},{5,4},{6,7},{7,6},{8,9},{9,8},{10,11... | collective-permute-start | bytes 983048 | tf_op jit(solution)/shard_map/ppermute | solution.py:15
  14.0 4.2 %resample.2 = (f32[640,128]{1,0:T(8,128)S(1)}, f32[640,128]{1,0:T(8,128)S(1)}, f32[640,128]{1,0:T(8,128)S(1)}) custom-call(s32[1,5]{1,0:T(1,128)S(1)} %copy-done.3, s32[1,5]{1,0:T(1,128)S(1)} %copy-done.4, s32[1,5]{1,0:T(1,128)S(1)} %copy-done.5, bf16[1,5,128,12]{3,2,1,0:T(8,128)(2,1)S(1)} %copy.13.coef_x, bf16[1,5,16,12]{3,2,1,0:T(8,128)(2,1)S(1)} %copy-done.1, ...), custom_call_target="tpu_custom_call" | custom-call | flops 581959680 | bytes 3276800 | tf_op jit(solution)/shard_map/resample/pallas_call | solution.py:105
  18.2 5.5 %collective-permute-done = f32[640,128]{1,0:T(8,128)S(1)} collective-permute-done((f32[640,128]{1,0:T(8,128)S(1)}, f32[640,128]{1,0:T(8,128)S(1)}, u32[]{:S(2)}, u32[]{:S(2)}) %collective-permute-start) | collective-permute-done | bytes 327712 | tf_op jit(solution)/shard_map/ppermute | solution.py:21
  23.7 0.1 collective-permute-start.1
  23.8 0.0 collective-permute-done.2
  23.9 4.2 %collective-permute-start.3 = (f32[640,128]{1,0:T(8,128)S(1)}, f32[640,128]{1,0:T(8,128)S(1)}, u32[]{:S(2)}, u32[]{:S(2)}) collective-permute-start(f32[640,128]{1,0:T(8,128)S(1)} %add.14), channel_id=1, source_target_pairs={{0,0},{1,2},{2,1},{3,4},{4,3},{5,6},{6,5},{7,8},{8,7},{9,10},{10,9... | collective-permute-start | bytes 983048 | tf_op jit(solution)/shard_map/ppermute | solution.py:21
  28.1 4.3 %collective-permute-done.1 = f32[640,128]{1,0:T(8,128)S(1)} collective-permute-done((f32[640,128]{1,0:T(8,128)S(1)}, f32[640,128]{1,0:T(8,128)S(1)}, u32[]{:S(2)}, u32[]{:S(2)}) %collective-permute-start.1) | collective-permute-done | bytes 327712 | tf_op jit(solution)/shard_map/ppermute | solution.py:15
  32.4 5.3 %collective-permute-done.3 = f32[640,128]{1,0:T(8,128)S(1)} collective-permute-done((f32[640,128]{1,0:T(8,128)S(1)}, f32[640,128]{1,0:T(8,128)S(1)}, u32[]{:S(2)}, u32[]{:S(2)}) %collective-permute-start.3) | collective-permute-done | bytes 327712 | tf_op jit(solution)/shard_map/ppermute | solution.py:21
  37.7 0.8 %add_add_fusion = f32[640,128]{1,0:T(8,128)} fusion(f32[640,128]{1,0:T(8,128)S(1)} %collective-permute-done.3, f32[640,128]{1,0:T(8,128)S(1)} %get-tuple-element.10, f32[640,128]{1,0:T(8,128)S(1)} %collective-permute-done.1), kind=kLoop, calls=%fused_computation | loop fusion | flops 163840 | bytes 1310720 | tf_op jit(solution)/shard_map/add | solution.py:185
  38.5 4.4 %all-to-all-start = ((f32[8,80,128]{2,1,0:T(8,128)}), f32[8,80,128]{2,1,0:T(8,128)S(1)}, u32[]{:S(2)}, u32[]{:S(2)}) async-start(f32[8,80,128]{2,1,0:T(8,128)} %bitcast), calls=%async_computation | async-start | bytes 655360 | tf_op jit(solution)/shard_map/all_to_all | solution.py:163
  42.9 0.1 copy.15.mask
  43.0 8.1 %all-to-all-done = f32[8,80,128]{2,1,0:T(8,128)S(1)} async-done(((f32[8,80,128]{2,1,0:T(8,128)}), f32[8,80,128]{2,1,0:T(8,128)S(1)}, u32[]{:S(2)}, u32[]{:S(2)}) %all-to-all-start) | async-done | bytes 327712 | tf_op jit(solution)/shard_map/all_to_all | solution.py:163
  51.1 1.3 %smooth.1 = f32[640,128]{1,0:T(8,128)} custom-call(s32[32,1]{1,0:T(8,128)S(1)} %copy.15.mask, f32[32,32]{1,0:T(8,128)S(1)} %copy-done.2, f32[640,128]{1,0:T(8,128)S(1)} %bitcast.3), custom_call_target="tpu_custom_call" | custom-call | tf_op jit(solution)/shard_map/smooth/pallas_call | solution.py:154
  (8 shorter events, 0.1 us)
Async XLA Ops:
  0.9 1.9 %copy-start = (bf16[4,10,80,512]{3,2,1,0:T(8,128)(2,1)S(1)}, bf16[4,10,80,512]{3,2,1,0:T(8,128)(2,1)}, u32[]{:S(2)}) copy-start(bf16[4,10,80,512]{3,2,1,0:T(8,128)(2,1)} %granule.3) | copy-start | bytes 9830404
  2.8 0.7 %copy-start.1 = (bf16[1,5,16,12]{3,2,1,0:T(8,128)(2,1)S(1)}, bf16[1,5,16,12]{3,2,1,0:T(8,128)(2,1)}, u32[]{:S(2)}) copy-start(bf16[1,5,16,12]{3,2,1,0:T(8,128)(2,1)} %coef_y.3) | copy-start | bytes 5764
  3.6 0.7 %copy-start.3 = (s32[1,5]{1,0:T(1,128)S(1)}, s32[1,5]{1,0:T(1,128)}, u32[]{:S(2)}) copy-start(s32[1,5]{1,0:T(1,128)} %targets.3) | copy-start | bytes 64
  4.2 0.7 %copy-start.4 = (s32[1,5]{1,0:T(1,128)S(1)}, s32[1,5]{1,0:T(1,128)}, u32[]{:S(2)}) copy-start(s32[1,5]{1,0:T(1,128)} %row_offset.3) | copy-start | bytes 64
  4.9 0.7 %copy-start.5 = (s32[1,5]{1,0:T(1,128)S(1)}, s32[1,5]{1,0:T(1,128)}, u32[]{:S(2)}) copy-start(s32[1,5]{1,0:T(1,128)} %col_offset.3) | copy-start | bytes 64
  9.0 14.7 %collective-permute-start = (f32[640,128]{1,0:T(8,128)S(1)}, f32[640,128]{1,0:T(8,128)S(1)}, u32[]{:S(2)}, u32[]{:S(2)}) collective-permute-start(f32[640,128]{1,0:T(8,128)S(1)} %get-tuple-element.12), channel_id=1, source_target_pairs={{0,0},{1,2},{2,1},{3,4},{4,3},{5,6},{6,5},{7,8},{8,7},{9,10},{10,9... | collective-permute-start | bytes 983048 | tf_op jit(solution)/shard_map/ppermute | solution.py:21
  13.2 29.7 %copy-start.6 = (s32[32,1]{0,1:T(1,128)S(1)}, s32[32,1]{0,1:T(1,128)}, u32[]{:S(2)}) copy-start(s32[32,1]{0,1:T(1,128)} %param.14) | copy-start | bytes 388
  13.2 37.9 %copy-start.2 = (f32[32,32]{1,0:T(8,128)S(1)}, f32[32,32]{1,0:T(8,128)}, u32[]{:S(2)}) copy-start(f32[32,32]{1,0:T(8,128)} %smoother.1) | copy-start | bytes 12292
  13.2 10.6 %collective-permute-start.2 = (f32[640,128]{1,0:T(8,128)S(1)}, f32[640,128]{1,0:T(8,128)S(1)}, u32[]{:S(2)}, u32[]{:S(2)}) collective-permute-start(f32[640,128]{1,0:T(8,128)S(1)} %get-tuple-element.14), channel_id=1, source_target_pairs={{0,1},{1,0},{2,3},{3,2},{4,5},{5,4},{6,7},{7,6},{8,9},{9,8},{10,11... | collective-permute-start | bytes 983048 | tf_op jit(solution)/shard_map/ppermute | solution.py:15
  23.7 8.7 %collective-permute-start.1 = (f32[640,128]{1,0:T(8,128)S(1)}, f32[640,128]{1,0:T(8,128)S(1)}, u32[]{:S(2)}, u32[]{:S(2)}) collective-permute-start(f32[640,128]{1,0:T(8,128)S(1)} %add.12), channel_id=1, source_target_pairs={{0,1},{1,0},{2,3},{3,2},{4,5},{5,4},{6,7},{7,6},{8,9},{9,8},{10,11... | collective-permute-start | bytes 983048 | tf_op jit(solution)/shard_map/ppermute | solution.py:15
  23.9 13.8 %collective-permute-start.3 = (f32[640,128]{1,0:T(8,128)S(1)}, f32[640,128]{1,0:T(8,128)S(1)}, u32[]{:S(2)}, u32[]{:S(2)}) collective-permute-start(f32[640,128]{1,0:T(8,128)S(1)} %add.14), channel_id=1, source_target_pairs={{0,0},{1,2},{2,1},{3,4},{4,3},{5,6},{6,5},{7,8},{8,7},{9,10},{10,9... | collective-permute-start | bytes 983048 | tf_op jit(solution)/shard_map/ppermute | solution.py:21
  38.5 12.6 %all-to-all-start = ((f32[8,80,128]{2,1,0:T(8,128)}), f32[8,80,128]{2,1,0:T(8,128)S(1)}, u32[]{:S(2)}, u32[]{:S(2)}) async-start(f32[8,80,128]{2,1,0:T(8,128)} %bitcast), calls=%async_computation | async-start | bytes 655360 | tf_op jit(solution)/shard_map/all_to_all | solution.py:163

commit v2 on v0

v2 whole, which is shorter than its diff:
```python
import functools

import jax
import jax.numpy as jnp
from jax import lax
from jax.experimental import pallas as pl
from jax.experimental.pallas import tpu as pltpu
from jax.sharding import PartitionSpec as P

HIGHEST = lax.Precision.HIGHEST
CHUNKS = (10,)


def even_swap(block):
    pairs = [(i, i ^ 1) for i in range(lax.axis_size("tile"))]
    return lax.ppermute(block, "tile", pairs)


def odd_swap(block):
    tiles = lax.axis_size("tile")
    pairs = []
    for date in range(lax.axis_size("date")):
        for tile in range(tiles):
            other, date_to = ((tile - 1) ^ 1) + 1, date
            if tile in (0, tiles - 1):
                other, date_to = tile, date ^ 1
            pairs.append((date * tiles + tile, date_to * tiles + other))
    return lax.ppermute(block, ("date", "tile"), pairs)


def date_swap(block, distance):
    return lax.ppermute(block, "date", [(i, i ^ distance) for i in range(lax.axis_size("date"))])


def resample_kernel(reaches, *refs):
    count = len(reaches)
    parts = count * len(CHUNKS)
    inputs, outs, scratch = refs[:6], refs[6 : 6 + parts], refs[6 + parts :]
    held, (x_mats, y_mats, sems, date_sems) = scratch[:6], scratch[6:]
    targets, row_offset, col_offset, coef_x, coef_y, granule = held
    slots, taps, tile_cols = coef_x.shape[1:]
    tile_rows = coef_y.shape[2]
    dates, bands, grid_rows, grid_cols = granule.shape

    small = [pltpu.make_async_copy(inputs[i], held[i], sems.at[i]) for i in range(5)]
    large = [
        pltpu.make_async_copy(inputs[5].at[d], granule.at[d], date_sems.at[d])
        for d in range(dates)
    ]
    for copy in small + large:
        copy.start()
    for copy in small:
        copy.wait()

    own = lax.axis_index("tile")
    side = 1 - 2 * lax.rem(own, 2)
    to_order = (
        lax.broadcasted_iota(jnp.int32, (tile_rows, tile_rows), 1)
        == 2 * lax.rem(lax.broadcasted_iota(jnp.int32, (tile_rows, tile_rows), 0), tile_rows // 2)
        + lax.broadcasted_iota(jnp.int32, (tile_rows, tile_rows), 0) // (tile_rows // 2)
    ).astype(jnp.float32)
    for n, reach in enumerate(reaches):
        wanted = own + side * reach
        slot = jnp.int32(0)
        used = jnp.int32(0)
        for k in range(slots):
            hit = jnp.logical_and(wanted >= 0, targets[0, k] == wanted).astype(jnp.int32)
            slot = slot + k * hit
            used = used + hit
        tap = (
            lax.broadcasted_iota(jnp.int32, (grid_cols, tile_cols), 0)
            - 2 * lax.broadcasted_iota(jnp.int32, (grid_cols, tile_cols), 1)
            - col_offset[0, slot]
        )
        coeffs = coef_x[0, slot].astype(jnp.float32)
        banded = jnp.zeros((grid_cols, tile_cols), jnp.float32)
        for t in range(taps):
            banded = jnp.where(tap == t, coeffs[t : t + 1, :], banded)
        x_mats[n] = banded.astype(jnp.bfloat16)
        tap = (
            lax.broadcasted_iota(jnp.int32, (tile_rows, grid_rows), 1)
            - 2 * lax.broadcasted_iota(jnp.int32, (tile_rows, grid_rows), 0)
            - row_offset[0, slot]
        )
        tap = jnp.where(used > 0, tap, -1)
        coeffs = coef_y[0, slot].astype(jnp.float32)
        banded = jnp.zeros((tile_rows, grid_rows), jnp.float32)
        for t in range(taps):
            banded = jnp.where(tap == t, coeffs[:, t : t + 1], banded)
        ordered = jnp.dot(to_order, banded, preferred_element_type=jnp.float32)
        y_mats[n * tile_rows : (n + 1) * tile_rows] = ordered.astype(jnp.bfloat16)

    half = tile_rows // 2
    for date in range(dates):
        large[date].wait()
        along_y = [
            jnp.dot(y_mats[...], granule[date, b], preferred_element_type=jnp.float32)
            for b in range(bands)
        ]
        for n in range(count):
            rows = jnp.concatenate([part[n * tile_rows : (n + 1) * tile_rows] for part in along_y], 0)
            high = rows.astype(jnp.bfloat16)
            low = (rows - high.astype(jnp.float32)).astype(jnp.bfloat16)
            both = jnp.dot(
                jnp.concatenate([high, low], 0), x_mats[n], preferred_element_type=jnp.float32
            )
            partial = both[: bands * tile_rows] + both[bands * tile_rows :]
            start = 0
            for c, width in enumerate(CHUNKS):
                out = outs[n * len(CHUNKS) + c]
                stride = out.shape[0] // half
                for b in range(width):
                    for parity in range(2):
                        first = (start + b) * tile_rows + parity * half
                        at = date * 2 * width + parity * width + b
                        out[pl.ds(at, half, stride=stride), :] = partial[first : first + half]
                start += width


def resample(reaches, limit, targets, row_offset, col_offset, coef_x, coef_y, granules):
    dates, bands, grid_rows, grid_cols = granules.shape
    taps, tile_cols = coef_x.shape[2:]
    tile_rows = coef_y.shape[2]
    count = len(reaches)
    shapes = [
        jax.ShapeDtypeStruct((dates * width * tile_rows, tile_cols), jnp.float32) for width in CHUNKS
    ] * count
    outs = pl.pallas_call(
        functools.partial(resample_kernel, reaches),
        in_specs=[pl.BlockSpec(memory_space=pltpu.HBM)] * 6,
        out_specs=[pl.BlockSpec(memory_space=pltpu.VMEM)] * len(shapes),
        out_shape=shapes,
        scratch_shapes=[
            pltpu.SMEM(targets.shape, jnp.int32),
            pltpu.SMEM(row_offset.shape, jnp.int32),
            pltpu.SMEM(col_offset.shape, jnp.int32),
            pltpu.VMEM(coef_x.shape, coef_x.dtype),
            pltpu.VMEM(coef_y.shape, coef_y.dtype),
            pltpu.VMEM((dates, bands, grid_rows, grid_cols), granules.dtype),
            pltpu.VMEM((count, grid_cols, tile_cols), jnp.bfloat16),
            pltpu.VMEM((count * tile_rows, grid_rows), jnp.bfloat16),
            pltpu.SemaphoreType.DMA((5,)),
            pltpu.SemaphoreType.DMA((dates,)),
        ],
        compiler_params=pltpu.CompilerParams(vmem_limit_bytes=limit),
        cost_estimate=pl.CostEstimate(
            flops=count * dates * bands * tile_rows * grid_cols * (grid_rows + 4 * tile_cols),
            bytes_accessed=granules.size * 2,
            transcendentals=0,
        ),
        name="resample",
    )(targets, row_offset, col_offset, coef_x, coef_y, granules)
    return [outs[c :: len(CHUNKS)] for c in range(len(CHUNKS))]


def weights_kernel(local_dates, mask, smoother, weights, totals):
    dates = smoother.shape[0]
    masked = smoother[...] * mask[...].astype(jnp.float32)
    me = lax.axis_index("date")
    source = lax.broadcasted_iota(jnp.int32, (dates, dates), 0)
    place = lax.broadcasted_iota(jnp.int32, (dates, dates), 1)
    wanted = ((place // local_dates) ^ me) * local_dates + lax.rem(place, local_dates)
    picks = (source == wanted).astype(jnp.float32)
    weights[...] = jnp.dot(masked, picks, precision=HIGHEST, preferred_element_type=jnp.float32)
    totals[...] = jnp.broadcast_to(jnp.sum(masked, 1, keepdims=True), totals.shape)


def smoothing_weights(local_dates, lanes, mask, smoother):
    return pl.pallas_call(
        functools.partial(weights_kernel, local_dates),
        out_shape=[
            jax.ShapeDtypeStruct(smoother.shape, jnp.float32),
            jax.ShapeDtypeStruct((smoother.shape[0], lanes), jnp.float32),
        ],
        compiler_params=pltpu.CompilerParams(vmem_limit_bytes=32 * 1024 * 1024),
        name="smoothing_weights",
    )(mask, smoother)


def smooth_kernel(pieces, weights, totals, *refs):
    series, out = refs[:-1], refs[-1]
    dates = weights.shape[0]
    stride = out.shape[0] // dates
    held = dates // pieces
    start = 0
    for c, bands in enumerate(CHUNKS):
        for b in range(bands):
            for parity in range(2):
                picked = jnp.concatenate(
                    [
                        part[pl.ds(parity * bands + b, held, stride=2 * bands), :]
                        for part in series[c * pieces : (c + 1) * pieces]
                    ],
                    0,
                )
                total = jnp.dot(
                    weights[...], picked, precision=HIGHEST, preferred_element_type=jnp.float32
                )
                at = 2 * (start + b) + parity
                out[pl.ds(at, dates, stride=stride), :] = total / totals[...]
        start += bands


def smooth(weights, totals, series):
    return pl.pallas_call(
        functools.partial(smooth_kernel, len(series[0])),
        out_shape=jax.ShapeDtypeStruct(
            (sum(part.shape[0] for chunk in series for part in chunk), totals.shape[1]), jnp.float32
        ),
        compiler_params=pltpu.CompilerParams(vmem_limit_bytes=32 * 1024 * 1024),
        name="smooth",
    )(weights, totals, *[part for chunk in series for part in chunk])


def to_pixel_blocks(terms):
    positions = lax.axis_size("date")
    me = lax.axis_index("date")
    core, y = lax.rem(me, 2), me // 2
    terms = [term.reshape(positions // 2, 2, -1, term.shape[-1]) for term in terms]

    def of_core(which):
        picked = [lax.dynamic_index_in_dim(term, which, 1, keepdims=False) for term in terms]
        return picked[0] + picked[1] + picked[2]

    mine, other = of_core(core), of_core(1 - core)
    got = date_swap(other, 1)
    blocks = []
    for distance in range(positions // 2):
        at = y ^ distance
        block = jnp.concatenate(
            [
                lax.dynamic_index_in_dim(mine, at, 0, keepdims=False),
                lax.dynamic_index_in_dim(got, at, 0, keepdims=False),
            ],
            0,
        )
        blocks.append(date_swap(block, 2 * distance) if distance else block)
    return blocks


def body(granules, coef_x, coef_y, row_offset, col_offset, targets, mask, smoother):
    local_dates, bands = granules.shape[:2]
    tile_cols = coef_x.shape[2]
    block_pix = tile_cols * coef_y.shape[2] // lax.axis_size("date")
    coef_x = jnp.transpose(coef_x, (0, 1, 3, 2))

    def run(reaches, limit):
        return resample(reaches, limit, targets, row_offset, col_offset, coef_x, coef_y, granules)

    weights, totals = smoothing_weights(local_dates, tile_cols, jnp.transpose(mask), smoother)
    far = run((2, -2), None)
    passed = [(even_swap(even), odd_swap(odd)) for even, odd in far]
    near = run((1, -1, 0), 32 * 1024 * 1024)
    arrived = [
        (even_swap(even + from_odd), odd_swap(odd + from_even))
        for (even, odd, _), (from_even, from_odd) in zip(near, passed)
    ]
    blocks = [to_pixel_blocks((own, even, odd)) for (_, _, own), (even, odd) in zip(near, arrived)]
    smoothed = smooth(weights, totals, blocks)
    return smoothed.reshape(smoother.shape[0], bands, 1, block_pix)


def solution(mesh):
    return jax.shard_map(
        body,
        mesh=mesh,
        in_specs=(
            P("date", None, "tile", None),
            P("tile", None, None, None),
            P("tile", None, None, None),
            P("tile", None),
            P("tile", None),
            P("tile", None),
            P(None, "tile"),
            P(),
        ),
        out_specs=P(None, None, "tile", "date"),
        check_vma=False,
    )
```

time: 155 us -> 44.4 us (0.29)
  matrix products: 51 us -> 0 us
  local copies, waits for them, and re-layouts: 51.5 us -> 0.79 us
  other arithmetic: 15.2 us -> 2 us
  Pallas kernels: 0 us -> 11.4 us
  starting transfers between devices: 17.7 us -> 9.81 us
  waiting for transfers between devices: 17.9 us -> 20 us
    dot_general x9 -> x0, matrix products: 51 us -> none  [the longest x1 24.8 us: body(): jnp.einsum('kir,dbrkj->kdbij', y_mats, x_pass, precision=lax.Precision.HI...]
    reshape x4 -> x0, local copies, waits for them, and re-layouts: 24.9 us -> none  [the longest x1 17.5 us: body(): x_pass.reshape(local_dates, band_count, grid_rows, slot_count, tile_cols)]
    unnamed x16 -> x18, local copies, waits for them, and re-layouts: 15.8 us -> 0.76 us
    pallas_call x0 -> x4, Pallas kernels: none -> 11.4 us  [the longest x2 10.1 us: resample(): pl.pallas_call(functools.partial(resample_kernel, reaches), in_specs=[pl....]
    ppermute x4 -> x8, waiting for transfers between devices: 9.67 us -> 20 us  [the longest x2 8.15 us: odd_swap(): return lax.ppermute(block, ('date', 'tile'), pairs)]
    all_to_all x1 -> x0, waiting for transfers between devices: 8.2 us -> none  [body(): lax.all_to_all(series, 'date', split_axis=2, concat_axis=0, tiled=True)]
    all_to_all x4 -> x0, local copies, waits for them, and re-layouts: 7.72 us -> none  [body(): lax.all_to_all(series, 'date', split_axis=2, concat_axis=0, tiled=True)]
    unnamed x8 -> x0, other arithmetic: 6.89 us -> none
  transfers between devices with their start and end apart: 5 -> 8, of which waited for: 3 -> 6; matrix products, arithmetic and copies ran while one was open for 10% -> 2% of each run, Pallas kernels for 0% -> 11%
where the time goes in v2:
time: 44.4 us; the launch traced here: 44.2 us
  waiting for transfers between devices  20 us (45%)
  Pallas kernels  11.4 us (26%)
  starting transfers between devices  9.81 us (22%)
  other arithmetic  2 us (5%)
  local copies, waits for them, and re-layouts  0.79 us (2%)
    pallas_call x2, Pallas kernels, resample(): pl.pallas_call(functools.partial(resample_kernel, reaches), in_specs=[pl....  10.1 us
    ppermute x2, waiting for transfers between devices, odd_swap(): return lax.ppermute(block, ('date', 'tile'), pairs)  8.15 us
    ppermute x2, waiting for transfers between devices, even_swap(): return lax.ppermute(block, 'tile', pairs)  5.96 us
    ppermute x4, waiting for transfers between devices, date_swap(): lax.ppermute(block, 'date', [(i, i ^ distance) for i in range(lax.axis_si...  5.91 us
    ppermute x2, starting transfers between devices, odd_swap(): return lax.ppermute(block, ('date', 'tile'), pairs)  4.76 us
    ppermute x4, starting transfers between devices, date_swap(): lax.ppermute(block, 'date', [(i, i ^ distance) for i in range(lax.axis_si...  4.27 us
    add x2, other arithmetic, of_core(): return picked[0] + picked[1] + picked[2]  1.9 us
    pallas_call x1, Pallas kernels, smooth(): pl.pallas_call(functools.partial(smooth_kernel, len(series[0])), out_shap...  1.22 us
  transfers between devices with their start and end apart: 8, of which 6 were waited for; matrix products, arithmetic and copies ran while one was open for 2% of the time, Pallas kernels for 11%

profile of v2, /device:TPU:128, one launch (start us, length us, event | category | flops | bytes accessed | tf_op | source)
XLA Modules:
  0.0 44.2 jit_solution(17388375946133637553)
XLA Ops:
  0.0 5.5 %resample.3 = (f32[640,128]{1,0:T(8,128)}, f32[640,128]{1,0:T(8,128)}) custom-call(s32[1,5]{1,0:T(1,128)} %refs_0_.3, s32[1,5]{1,0:T(1,128)} %refs_1_.3, s32[1,5]{1,0:T(1,128)} %refs_2_.3, bf16[1,5,12,128]{3,2,1,0:T(8,128)(2,1)} %bitcast.36, bf16[1,5,16,12]{3,2,1,0:T(8,128)(2,1)} %refs_4_.3, bf16[4,10,80,512]{3,2,1,0:T(8,128)(2,1)} %refs_5_.3), custom_call_target="tpu_custom_call" | custom-call | flops 387973120 | bytes 3276800 | tf_op jit(solution)/shard_map/resample/pallas_call | solution.py:128
  5.5 0.0 copy-start.4
  5.6 0.0 copy-start.8
  5.6 2.4 %collective-permute-start = (f32[640,128]{1,0:T(8,128)}, f32[640,128]{1,0:T(8,128)S(1)}, u32[]{:S(2)}, u32[]{:S(2)}) collective-permute-start(f32[640,128]{1,0:T(8,128)} %get-tuple-element.16), channel_id=1, source_target_pairs={{0,32},{1,2},{2,1},{3,4},{4,3},{5,6},{6,5},{7,8},{8,7},{9,10},{10,... | collective-permute-start | bytes 983048 | tf_op jit(solution)/shard_map/ppermute | solution.py:28
  7.9 0.7 %collective-permute-start.2 = (f32[640,128]{1,0:T(8,128)}, f32[640,128]{1,0:T(8,128)S(1)}, u32[]{:S(2)}, u32[]{:S(2)}) collective-permute-start(f32[640,128]{1,0:T(8,128)} %get-tuple-element.18), channel_id=1, source_target_pairs={{0,1},{1,0},{2,3},{3,2},{4,5},{5,4},{6,7},{7,6},{8,9},{9,8},{10,11... | collective-permute-start | bytes 983048 | tf_op jit(solution)/shard_map/ppermute | solution.py:16
  8.7 4.6 %resample.2 = (f32[640,128]{1,0:T(8,128)S(1)}, f32[640,128]{1,0:T(8,128)S(1)}, f32[640,128]{1,0:T(8,128)S(1)}) custom-call(s32[1,5]{1,0:T(1,128)S(1)} %copy-done.5, s32[1,5]{1,0:T(1,128)S(1)} %copy-done.6, s32[1,5]{1,0:T(1,128)S(1)} %copy-done.7, bf16[1,5,12,128]{3,2,1,0:T(8,128)(2,1)S(1)} %bitcast.37, bf16[1,5,16,12]{3,2,1,0:T(8,128)(2,1)S(1)} %copy-done.3, ...), custom_call_target="tpu_custom_call" | custom-call | flops 581959680 | bytes 3276800 | tf_op jit(solution)/shard_map/resample/pallas_call | solution.py:128
  13.2 0.7 %copy-done.1 = f32[640,128]{1,0:T(8,128)} copy-done((f32[640,128]{1,0:T(8,128)}, f32[640,128]{1,0:T(8,128)S(1)}, u32[]{:S(2)}) %copy-start.1) | copy-done | bytes 327704
  14.0 4.7 %collective-permute-done = f32[640,128]{1,0:T(8,128)S(1)} collective-permute-done((f32[640,128]{1,0:T(8,128)}, f32[640,128]{1,0:T(8,128)S(1)}, u32[]{:S(2)}, u32[]{:S(2)}) %collective-permute-start) | collective-permute-done | bytes 327712 | tf_op jit(solution)/shard_map/ppermute | solution.py:28
  18.7 0.1 collective-permute-start.1
  18.8 2.4 %collective-permute-start.3 = (f32[640,128]{1,0:T(8,128)S(1)}, f32[640,128]{1,0:T(8,128)S(1)}, u32[]{:S(2)}, u32[]{:S(2)}) collective-permute-start(f32[640,128]{1,0:T(8,128)S(1)} %add.57), channel_id=1, source_target_pairs={{0,32},{1,2},{2,1},{3,4},{4,3},{5,6},{6,5},{7,8},{8,7},{9,10},{10,... | collective-permute-start | bytes 983048 | tf_op jit(solution)/shard_map/ppermute | solution.py:28
  21.2 0.1 smoothing_weights.1
  21.4 6.0 %collective-permute-done.1 = f32[640,128]{1,0:T(8,128)S(1)} collective-permute-done((f32[640,128]{1,0:T(8,128)S(1)}, f32[640,128]{1,0:T(8,128)S(1)}, u32[]{:S(2)}, u32[]{:S(2)}) %collective-permute-start.1) | collective-permute-done | bytes 327712 | tf_op jit(solution)/shard_map/ppermute | solution.py:16
  27.3 3.5 %collective-permute-done.3 = f32[640,128]{1,0:T(8,128)S(1)} collective-permute-done((f32[640,128]{1,0:T(8,128)S(1)}, f32[640,128]{1,0:T(8,128)S(1)}, u32[]{:S(2)}, u32[]{:S(2)}) %collective-permute-start.3) | collective-permute-done | bytes 327712 | tf_op jit(solution)/shard_map/ppermute | solution.py:28
  30.8 1.0 %fusion = f32[4,80,128]{2,1,0:T(8,128)S(1)} fusion(f32[4,2,80,128]{3,2,1,0:T(8,128)S(1)} %bitcast.41, s32[]{:T(128)S(6)} %select_n.36, f32[4,2,80,128]{3,2,1,0:T(8,128)S(1)} %bitcast.39, f32[4,2,80,128]{3,2,1,0:T(8,128)} %bitcast.34), kind=kLoop, calls=%fused_computation.1 | loop fusion | flops 81920 | bytes 655364 | tf_op jit(solution)/shard_map/add | solution.py:223
  31.7 0.1 collective-permute-start.4
  31.8 1.0 %dynamic-slice_add_fusion = f32[4,1,80,128]{3,2,1,0:T(8,128)S(1)} fusion(f32[4,2,80,128]{3,2,1,0:T(8,128)S(1)} %bitcast.42, s32[]{:T(128)S(6)} %select_n.33, f32[4,2,80,128]{3,2,1,0:T(8,128)S(1)} %bitcast.40, f32[4,2,80,128]{3,2,1,0:T(8,128)} %bitcast.35), kind=kLoop, calls=%fused_computation.3 | loop fusion | flops 81920 | bytes 655364 | tf_op jit(solution)/shard_map/add | solution.py:223
  32.8 0.4 collective-permute-done.4
  33.3 3.1 %collective-permute-start.7 = (f32[160,128]{1,0:T(8,128)S(1)}, f32[160,128]{1,0:T(8,128)S(1)}, u32[]{:S(2)}, u32[]{:S(2)}) collective-permute-start(f32[160,128]{1,0:T(8,128)S(1)} %pad_maximum_fusion.3), channel_id=1, source_target_pairs={{0,192},{32,224},{64,128},{96,160},{128,64},{160,96},{192,0},{224,... | collective-permute-start | bytes 245768 | tf_op jit(solution)/shard_map/ppermute | solution.py:32
  36.4 0.6 %collective-permute-start.6 = (f32[160,128]{1,0:T(8,128)S(1)}, f32[160,128]{1,0:T(8,128)S(1)}, u32[]{:S(2)}, u32[]{:S(2)}) collective-permute-start(f32[160,128]{1,0:T(8,128)S(1)} %pad_maximum_fusion.2), channel_id=1, source_target_pairs={{0,128},{32,160},{64,192},{96,224},{128,0},{160,32},{192,64},{224,... | collective-permute-start | bytes 245768 | tf_op jit(solution)/shard_map/ppermute | solution.py:32
  37.0 0.4 collective-permute-start.5
  37.5 2.7 %collective-permute-done.7.refs_3_ = f32[160,128]{1,0:T(8,128)S(1)} collective-permute-done((f32[160,128]{1,0:T(8,128)S(1)}, f32[160,128]{1,0:T(8,128)S(1)}, u32[]{:S(2)}, u32[]{:S(2)}) %collective-permute-start.7) | collective-permute-done | bytes 81952 | tf_op jit(solution)/shard_map/ppermute | solution.py:32
  40.2 2.8 %collective-permute-done.6.refs_2_ = f32[160,128]{1,0:T(8,128)S(1)} collective-permute-done((f32[160,128]{1,0:T(8,128)S(1)}, f32[160,128]{1,0:T(8,128)S(1)}, u32[]{:S(2)}, u32[]{:S(2)}) %collective-permute-start.6) | collective-permute-done | bytes 81952 | tf_op jit(solution)/shard_map/ppermute | solution.py:32
  43.0 0.0 collective-permute-done.5.refs_1_
  43.0 1.2 %smooth.1 = f32[640,128]{1,0:T(8,128)} custom-call(f32[32,32]{1,0:T(8,128)S(1)} %get-tuple-element.12.weights, f32[32,128]{1,0:T(8,128)S(1)} %get-tuple-element.13.totals, f32[160,128]{1,0:T(8,128)S(1)} %pad_maximum_fusion.refs_0_, f32[160,128]{1,0:T(8,128)S(1)} %collective-permute-done.5.refs_1_, f32[160,128]{1,0:T(8,128)S(1)} %collective-permute-done.6.refs_2_, ...), custom_call_target="tpu_custom_call" | custom-call | tf_op jit(solution)/shard_map/smooth/pallas_call | solution.py:205
  (24 shorter events, 0.2 us)
Async XLA Ops:
  0.0 8.6 %copy-start.2 = (bf16[1,5,128,12]{2,3,1,0:T(8,128)(2,1)S(1)}, bf16[1,5,128,12]{2,3,1,0:T(8,128)(2,1)}, u32[]{:S(2)}) copy-start(bf16[1,5,128,12]{2,3,1,0:T(8,128)(2,1)} %param.9) | copy-start | bytes 46084
  0.0 8.6 %copy-start.3 = (bf16[1,5,16,12]{3,2,1,0:T(8,128)(2,1)S(1)}, bf16[1,5,16,12]{3,2,1,0:T(8,128)(2,1)}, u32[]{:S(2)}) copy-start(bf16[1,5,16,12]{3,2,1,0:T(8,128)(2,1)} %refs_4_.3) | copy-start | bytes 5764
  0.0 8.6 %copy-start.6 = (s32[1,5]{1,0:T(1,128)S(1)}, s32[1,5]{1,0:T(1,128)}, u32[]{:S(2)}) copy-start(s32[1,5]{1,0:T(1,128)} %refs_1_.3) | copy-start | bytes 64
  0.0 8.6 %copy-start.7 = (s32[1,5]{1,0:T(1,128)S(1)}, s32[1,5]{1,0:T(1,128)}, u32[]{:S(2)}) copy-start(s32[1,5]{1,0:T(1,128)} %refs_2_.3) | copy-start | bytes 64
  0.0 8.6 %copy-start.5 = (s32[1,5]{1,0:T(1,128)S(1)}, s32[1,5]{1,0:T(1,128)}, u32[]{:S(2)}) copy-start(s32[1,5]{1,0:T(1,128)} %refs_0_.3) | copy-start | bytes 64
  0.0 8.6 %copy-start = (bf16[4,10,80,512]{3,2,1,0:T(8,128)(2,1)S(1)}, bf16[4,10,80,512]{3,2,1,0:T(8,128)(2,1)}, u32[]{:S(2)}) copy-start(bf16[4,10,80,512]{3,2,1,0:T(8,128)(2,1)} %refs_5_.3) | copy-start | bytes 9830404
  5.5 15.7 %copy-start.4 = (f32[32,32]{1,0:T(8,128)S(1)}, f32[32,32]{1,0:T(8,128)}, u32[]{:S(2)}) copy-start(f32[32,32]{1,0:T(8,128)} %smoother.1) | copy-start | bytes 12292
  5.6 15.7 %copy-start.8 = (s32[32,1]{0,1:T(1,128)S(1)}, s32[32,1]{0,1:T(1,128)}, u32[]{:S(2)}) copy-start(s32[32,1]{0,1:T(1,128)} %param.14) | copy-start | bytes 388
  5.6 13.1 %collective-permute-start = (f32[640,128]{1,0:T(8,128)}, f32[640,128]{1,0:T(8,128)S(1)}, u32[]{:S(2)}, u32[]{:S(2)}) collective-permute-start(f32[640,128]{1,0:T(8,128)} %get-tuple-element.16), channel_id=1, source_target_pairs={{0,32},{1,2},{2,1},{3,4},{4,3},{5,6},{6,5},{7,8},{8,7},{9,10},{10,... | collective-permute-start | bytes 983048 | tf_op jit(solution)/shard_map/ppermute | solution.py:28
  7.9 10.8 %collective-permute-start.2 = (f32[640,128]{1,0:T(8,128)}, f32[640,128]{1,0:T(8,128)S(1)}, u32[]{:S(2)}, u32[]{:S(2)}) collective-permute-start(f32[640,128]{1,0:T(8,128)} %get-tuple-element.18), channel_id=1, source_target_pairs={{0,1},{1,0},{2,3},{3,2},{4,5},{5,4},{6,7},{7,6},{8,9},{9,8},{10,11... | collective-permute-start | bytes 983048 | tf_op jit(solution)/shard_map/ppermute | solution.py:16
  13.2 0.7 %copy-start.1 = (f32[640,128]{1,0:T(8,128)}, f32[640,128]{1,0:T(8,128)S(1)}, u32[]{:S(2)}) copy-start(f32[640,128]{1,0:T(8,128)S(1)} %get-tuple-element.14) | copy-start | bytes 983044
  18.7 8.6 %collective-permute-start.1 = (f32[640,128]{1,0:T(8,128)S(1)}, f32[640,128]{1,0:T(8,128)S(1)}, u32[]{:S(2)}, u32[]{:S(2)}) collective-permute-start(f32[640,128]{1,0:T(8,128)S(1)} %add.55), channel_id=1, source_target_pairs={{0,1},{1,0},{2,3},{3,2},{4,5},{5,4},{6,7},{7,6},{8,9},{9,8},{10,11... | collective-permute-start | bytes 983048 | tf_op jit(solution)/shard_map/ppermute | solution.py:16
  18.8 12.0 %collective-permute-start.3 = (f32[640,128]{1,0:T(8,128)S(1)}, f32[640,128]{1,0:T(8,128)S(1)}, u32[]{:S(2)}, u32[]{:S(2)}) collective-permute-start(f32[640,128]{1,0:T(8,128)S(1)} %add.57), channel_id=1, source_target_pairs={{0,32},{1,2},{2,1},{3,4},{4,3},{5,6},{6,5},{7,8},{8,7},{9,10},{10,... | collective-permute-start | bytes 983048 | tf_op jit(solution)/shard_map/ppermute | solution.py:28
  31.7 1.5 %collective-permute-start.4 = (f32[4,80,128]{2,1,0:T(8,128)S(1)}, f32[4,80,128]{2,1,0:T(8,128)S(1)}, u32[]{:S(2)}, u32[]{:S(2)}) collective-permute-start(f32[4,80,128]{2,1,0:T(8,128)S(1)} %fusion), channel_id=1, source_target_pairs={{0,32},{32,0},{64,96},{96,64},{128,160},{160,128},{192,224},{224,1... | collective-permute-start | bytes 491528 | tf_op jit(solution)/shard_map/ppermute | solution.py:32
  33.3 6.9 %collective-permute-start.7 = (f32[160,128]{1,0:T(8,128)S(1)}, f32[160,128]{1,0:T(8,128)S(1)}, u32[]{:S(2)}, u32[]{:S(2)}) collective-permute-start(f32[160,128]{1,0:T(8,128)S(1)} %pad_maximum_fusion.3), channel_id=1, source_target_pairs={{0,192},{32,224},{64,128},{96,160},{128,64},{160,96},{192,0},{224,... | collective-permute-start | bytes 245768 | tf_op jit(solution)/shard_map/ppermute | solution.py:32
  36.4 6.6 %collective-permute-start.6 = (f32[160,128]{1,0:T(8,128)S(1)}, f32[160,128]{1,0:T(8,128)S(1)}, u32[]{:S(2)}, u32[]{:S(2)}) collective-permute-start(f32[160,128]{1,0:T(8,128)S(1)} %pad_maximum_fusion.2), channel_id=1, source_target_pairs={{0,128},{32,160},{64,192},{96,224},{128,0},{160,32},{192,64},{224,... | collective-permute-start | bytes 245768 | tf_op jit(solution)/shard_map/ppermute | solution.py:32
  37.0 6.0 %collective-permute-start.5 = (f32[160,128]{1,0:T(8,128)S(1)}, f32[160,128]{1,0:T(8,128)S(1)}, u32[]{:S(2)}, u32[]{:S(2)}) collective-permute-start(f32[160,128]{1,0:T(8,128)S(1)} %pad_maximum_fusion.1), channel_id=1, source_target_pairs={{0,64},{32,96},{64,0},{96,32},{128,192},{160,224},{192,128},{224,1... | collective-permute-start | bytes 245768 | tf_op jit(solution)/shard_map/ppermute | solution.py:32

commit v3 on v2

--- a/solution.py
+++ b/solution.py
@@ -9,6 +9,7 @@
 
 HIGHEST = lax.Precision.HIGHEST
 CHUNKS = (10,)
+LIMIT = 12 * 1024 * 1024
 
 
 def even_swap(block):
@@ -32,10 +33,11 @@
     return lax.ppermute(block, "date", [(i, i ^ distance) for i in range(lax.axis_size("date"))])
 
 
-def resample_kernel(reaches, *refs):
+def resample_kernel(reaches, extra, *refs):
     count = len(reaches)
     parts = count * len(CHUNKS)
-    inputs, outs, scratch = refs[:6], refs[6 : 6 + parts], refs[6 + parts :]
+    inputs, refs = refs[:6], refs[6 + extra :]
+    outs, scratch = refs[:parts], refs[parts + extra // 2 :]
     held, (x_mats, y_mats, sems, date_sems) = scratch[:6], scratch[6:]
     targets, row_offset, col_offset, coef_x, coef_y, granule = held
     slots, taps, tile_cols = coef_x.shape[1:]
@@ -117,7 +119,7 @@
                 start += width
 
 
-def resample(reaches, limit, targets, row_offset, col_offset, coef_x, coef_y, granules):
+def resample(reaches, limit, targets, row_offset, col_offset, coef_x, coef_y, granules, after=(), passed_on=()):
     dates, bands, grid_rows, grid_cols = granules.shape
     taps, tile_cols = coef_x.shape[2:]
     tile_rows = coef_y.shape[2]
@@ -126,10 +128,13 @@
         jax.ShapeDtypeStruct((dates * width * tile_rows, tile_cols), jnp.float32) for width in CHUNKS
     ] * count
     outs = pl.pallas_call(
-        functools.partial(resample_kernel, reaches),
-        in_specs=[pl.BlockSpec(memory_space=pltpu.HBM)] * 6,
-        out_specs=[pl.BlockSpec(memory_space=pltpu.VMEM)] * len(shapes),
-        out_shape=shapes,
+        functools.partial(resample_kernel, reaches, len(after) + len(passed_on)),
+        in_specs=[pl.BlockSpec(memory_space=pltpu.HBM)] * 6
+        + [pl.BlockSpec(memory_space=pl.ANY)] * (len(after) + len(passed_on)),
+        out_specs=[pl.BlockSpec(memory_space=pltpu.VMEM)] * len(shapes)
+        + [pl.BlockSpec(memory_space=pl.ANY)] * len(passed_on),
+        out_shape=shapes + [jax.ShapeDtypeStruct(array.shape, array.dtype) for array in passed_on],
+        input_output_aliases={6 + len(after) + i: len(shapes) + i for i in range(len(passed_on))},
         scratch_shapes=[
             pltpu.SMEM(targets.shape, jnp.int32),
             pltpu.SMEM(row_offset.shape, jnp.int32),
@@ -149,7 +154,9 @@
             transcendentals=0,
         ),
         name="resample",
-    )(targets, row_offset, col_offset, coef_x, coef_y, granules)
+    )(targets, row_offset, col_offset, coef_x, coef_y, granules, *after, *passed_on)
+    if passed_on:
+        return outs
     return [outs[c :: len(CHUNKS)] for c in range(len(CHUNKS))]
 
 
@@ -172,7 +179,7 @@
             jax.ShapeDtypeStruct(smoother.shape, jnp.float32),
             jax.ShapeDtypeStruct((smoother.shape[0], lanes), jnp.float32),
         ],
-        compiler_params=pltpu.CompilerParams(vmem_limit_bytes=32 * 1024 * 1024),
+        compiler_params=pltpu.CompilerParams(vmem_limit_bytes=LIMIT),
         name="smoothing_weights",
     )(mask, smoother)
 
@@ -207,7 +214,7 @@
         out_shape=jax.ShapeDtypeStruct(
             (sum(part.shape[0] for chunk in series for part in chunk), totals.shape[1]), jnp.float32
         ),
-        compiler_params=pltpu.CompilerParams(vmem_limit_bytes=32 * 1024 * 1024),
+        compiler_params=pltpu.CompilerParams(vmem_limit_bytes=LIMIT),
         name="smooth",
     )(weights, totals, *[part for chunk in series for part in chunk])
 
@@ -244,18 +251,15 @@
     block_pix = tile_cols * coef_y.shape[2] // lax.axis_size("date")
     coef_x = jnp.transpose(coef_x, (0, 1, 3, 2))
 
-    def run(reaches, limit):
-        return resample(reaches, limit, targets, row_offset, col_offset, coef_x, coef_y, granules)
-
+    operands = (targets, row_offset, col_offset, coef_x, coef_y, granules)
     weights, totals = smoothing_weights(local_dates, tile_cols, jnp.transpose(mask), smoother)
-    far = run((2, -2), None)
-    passed = [(even_swap(even), odd_swap(odd)) for even, odd in far]
-    near = run((1, -1, 0), 32 * 1024 * 1024)
-    arrived = [
-        (even_swap(even + from_odd), odd_swap(odd + from_even))
-        for (even, odd, _), (from_even, from_odd) in zip(near, passed)
-    ]
-    blocks = [to_pixel_blocks((own, even, odd)) for (_, _, own), (even, odd) in zip(near, arrived)]
+    ((far_even, far_odd),) = resample((2, -2), 56 * 1024 * 1024, *operands)
+    from_odd = odd_swap(far_odd)
+    from_even = even_swap(far_even)
+    ((even, odd, own),) = resample((1, -1, 0), LIMIT, *operands)
+    arrived_odd = odd_swap(odd + from_even)
+    arrived_even = even_swap(even + from_odd)
+    blocks = [to_pixel_blocks((own, arrived_odd, arrived_even))]
     smoothed = smooth(weights, totals, blocks)
     return smoothed.reshape(smoother.shape[0], bands, 1, block_pix)
 

time: 44.4 us -> 40.8 us (0.919)
  other arithmetic: 2 us -> 0.21 us
  waiting for transfers between devices: 20 us -> 18.9 us
  local copies, waits for them, and re-layouts: 0.79 us -> 0.07 us
    ppermute x2, waiting for transfers between devices: 5.96 us -> 2.87 us  [even_swap(): return lax.ppermute(block, 'tile', pairs)]
    add x2, other arithmetic: 1.9 us -> 0.09 us  [of_core(): return picked[0] + picked[1] + picked[2]]
    ppermute x2, waiting for transfers between devices: 8.15 us -> 9.24 us  [odd_swap(): return lax.ppermute(block, ('date', 'tile'), pairs)]
    ppermute x2, starting transfers between devices: 0.77 us -> 1.67 us  [even_swap(): return lax.ppermute(block, 'tile', pairs)]
    ppermute x4, waiting for transfers between devices: 5.91 us -> 6.78 us  [date_swap(): lax.ppermute(block, 'date', [(i, i ^ distance) for i in range(lax.axis_si...]
    ppermute x2, starting transfers between devices: 4.76 us -> 4.03 us  [odd_swap(): return lax.ppermute(block, ('date', 'tile'), pairs)]
    unnamed x18 -> x16, local copies, waits for them, and re-layouts: 0.76 us -> 0.04 us
  transfers between devices with their start and end apart: 8 -> 8, of which waited for: 6 -> 7; matrix products, arithmetic and copies ran while one was open for 2% -> 0% of each run, Pallas kernels for 11% -> 11%
where the time goes in v3:
time: 40.8 us; the launch traced here: 40.7 us
  waiting for transfers between devices  18.9 us (46%)
  Pallas kernels  11.4 us (28%)
  starting transfers between devices  9.97 us (24%)
    pallas_call x2, Pallas kernels, resample(): pl.pallas_call(functools.partial(resample_kernel, reaches, len(after) + l...  10 us
    ppermute x2, waiting for transfers between devices, odd_swap(): return lax.ppermute(block, ('date', 'tile'), pairs)  9.24 us
    ppermute x4, waiting for transfers between devices, date_swap(): lax.ppermute(block, 'date', [(i, i ^ distance) for i in range(lax.axis_si...  6.78 us
    ppermute x4, starting transfers between devices, date_swap(): lax.ppermute(block, 'date', [(i, i ^ distance) for i in range(lax.axis_si...  4.27 us
    ppermute x2, starting transfers between devices, odd_swap(): return lax.ppermute(block, ('date', 'tile'), pairs)  4.03 us
    ppermute x2, waiting for transfers between devices, even_swap(): return lax.ppermute(block, 'tile', pairs)  2.87 us
    ppermute x2, starting transfers between devices, even_swap(): return lax.ppermute(block, 'tile', pairs)  1.67 us
    pallas_call x1, Pallas kernels, smooth(): pl.pallas_call(functools.partial(smooth_kernel, len(series[0])), out_shap...  1.22 us
  transfers between devices with their start and end apart: 8, of which 7 were waited for; matrix products, arithmetic and copies ran while one was open for 0% of the time, Pallas kernels for 11%

profile of v3, /device:TPU:128, one launch (start us, length us, event | category | flops | bytes accessed | tf_op | source)
XLA Modules:
  0.0 40.7 jit_solution(14103575295133225279)
XLA Ops:
  0.0 0.0 copy-start.6
  0.0 0.0 copy-start.4
  0.0 5.5 %resample.3 = (f32[640,128]{1,0:T(8,128)}, f32[640,128]{1,0:T(8,128)}) custom-call(s32[1,5]{1,0:T(1,128)} %refs_0_.3, s32[1,5]{1,0:T(1,128)} %refs_1_.3, s32[1,5]{1,0:T(1,128)} %refs_2_.3, bf16[1,5,12,128]{3,2,1,0:T(8,128)(2,1)} %bitcast.36, bf16[1,5,16,12]{3,2,1,0:T(8,128)(2,1)} %refs_4_.3, bf16[4,10,80,512]{3,2,1,0:T(8,128)(2,1)} %refs_5_.3), custom_call_target="tpu_custom_call" | custom-call | flops 387973120 | bytes 3276800 | tf_op jit(solution)/shard_map/resample/pallas_call | solution.py:130
  5.5 0.0 copy-start.3
  5.6 0.0 copy-start.7
  5.6 1.6 %collective-permute-start = (f32[640,128]{1,0:T(8,128)}, f32[640,128]{1,0:T(8,128)S(1)}, u32[]{:S(2)}, u32[]{:S(2)}) collective-permute-start(f32[640,128]{1,0:T(8,128)} %get-tuple-element.16), channel_id=1, source_target_pairs={{0,1},{1,0},{2,3},{3,2},{4,5},{5,4},{6,7},{7,6},{8,9},{9,8},{10,11... | collective-permute-start | bytes 983048 | tf_op jit(solution)/shard_map/ppermute | solution.py:17
  7.1 1.6 %collective-permute-start.2 = (f32[640,128]{1,0:T(8,128)}, f32[640,128]{1,0:T(8,128)S(1)}, u32[]{:S(2)}, u32[]{:S(2)}) collective-permute-start(f32[640,128]{1,0:T(8,128)} %get-tuple-element.18), channel_id=1, source_target_pairs={{0,32},{1,2},{2,1},{3,4},{4,3},{5,6},{6,5},{7,8},{8,7},{9,10},{10,... | collective-permute-start | bytes 983048 | tf_op jit(solution)/shard_map/ppermute | solution.py:29
  8.8 4.5 %resample.2 = (f32[640,128]{1,0:T(8,128)S(1)}, f32[640,128]{1,0:T(8,128)S(1)}, f32[640,128]{1,0:T(8,128)S(1)}) custom-call(s32[1,5]{1,0:T(1,128)S(1)} %copy-done.4, s32[1,5]{1,0:T(1,128)S(1)} %copy-done.5, s32[1,5]{1,0:T(1,128)S(1)} %copy-done.6, bf16[1,5,12,128]{3,2,1,0:T(8,128)(2,1)S(1)} %bitcast.37, bf16[1,5,16,12]{3,2,1,0:T(8,128)(2,1)S(1)} %copy-done.2, ...), custom_call_target="tpu_custom_call" | custom-call | flops 581959680 | bytes 3276800 | tf_op jit(solution)/shard_map/resample/pallas_call | solution.py:130
  13.4 2.0 %collective-permute-done = f32[640,128]{1,0:T(8,128)S(1)} collective-permute-done((f32[640,128]{1,0:T(8,128)}, f32[640,128]{1,0:T(8,128)S(1)}, u32[]{:S(2)}, u32[]{:S(2)}) %collective-permute-start) | collective-permute-done | bytes 327712 | tf_op jit(solution)/shard_map/ppermute | solution.py:17
  15.4 2.4 %collective-permute-start.1 = (f32[640,128]{1,0:T(8,128)S(1)}, f32[640,128]{1,0:T(8,128)S(1)}, u32[]{:S(2)}, u32[]{:S(2)}) collective-permute-start(f32[640,128]{1,0:T(8,128)S(1)} %add.55), channel_id=1, source_target_pairs={{0,32},{1,2},{2,1},{3,4},{4,3},{5,6},{6,5},{7,8},{8,7},{9,10},{10,... | collective-permute-start | bytes 983048 | tf_op jit(solution)/shard_map/ppermute | solution.py:29
  17.7 2.1 %collective-permute-done.2 = f32[640,128]{1,0:T(8,128)S(1)} collective-permute-done((f32[640,128]{1,0:T(8,128)}, f32[640,128]{1,0:T(8,128)S(1)}, u32[]{:S(2)}, u32[]{:S(2)}) %collective-permute-start.2) | collective-permute-done | bytes 327712 | tf_op jit(solution)/shard_map/ppermute | solution.py:29
  19.9 0.1 collective-permute-start.3
  20.1 0.1 smoothing_weights.1
  20.2 7.1 %collective-permute-done.1 = f32[640,128]{1,0:T(8,128)S(1)} collective-permute-done((f32[640,128]{1,0:T(8,128)S(1)}, f32[640,128]{1,0:T(8,128)S(1)}, u32[]{:S(2)}, u32[]{:S(2)}) %collective-permute-start.1) | collective-permute-done | bytes 327712 | tf_op jit(solution)/shard_map/ppermute | solution.py:29
  27.3 0.9 %collective-permute-done.3 = f32[640,128]{1,0:T(8,128)S(1)} collective-permute-done((f32[640,128]{1,0:T(8,128)S(1)}, f32[640,128]{1,0:T(8,128)S(1)}, u32[]{:S(2)}, u32[]{:S(2)}) %collective-permute-start.3) | collective-permute-done | bytes 327712 | tf_op jit(solution)/shard_map/ppermute | solution.py:17
  28.3 0.1 collective-permute-start.4
  28.5 1.3 %collective-permute-done.4 = f32[4,80,128]{2,1,0:T(8,128)S(1)} collective-permute-done((f32[4,80,128]{2,1,0:T(8,128)S(1)}, f32[4,80,128]{2,1,0:T(8,128)S(1)}, u32[]{:S(2)}, u32[]{:S(2)}) %collective-permute-start.4) | collective-permute-done | bytes 163872 | tf_op jit(solution)/shard_map/ppermute | solution.py:33
  29.8 3.1 %collective-permute-start.7 = (f32[160,128]{1,0:T(8,128)S(1)}, f32[160,128]{1,0:T(8,128)S(1)}, u32[]{:S(2)}, u32[]{:S(2)}) collective-permute-start(f32[160,128]{1,0:T(8,128)S(1)} %pad_maximum_fusion.3), channel_id=1, source_target_pairs={{0,192},{32,224},{64,128},{96,160},{128,64},{160,96},{192,0},{224,... | collective-permute-start | bytes 245768 | tf_op jit(solution)/shard_map/ppermute | solution.py:33
  32.9 0.6 %collective-permute-start.6 = (f32[160,128]{1,0:T(8,128)S(1)}, f32[160,128]{1,0:T(8,128)S(1)}, u32[]{:S(2)}, u32[]{:S(2)}) collective-permute-start(f32[160,128]{1,0:T(8,128)S(1)} %pad_maximum_fusion.2), channel_id=1, source_target_pairs={{0,128},{32,160},{64,192},{96,224},{128,0},{160,32},{192,64},{224,... | collective-permute-start | bytes 245768 | tf_op jit(solution)/shard_map/ppermute | solution.py:33
  33.5 0.5 %collective-permute-start.5 = (f32[160,128]{1,0:T(8,128)S(1)}, f32[160,128]{1,0:T(8,128)S(1)}, u32[]{:S(2)}, u32[]{:S(2)}) collective-permute-start(f32[160,128]{1,0:T(8,128)S(1)} %pad_maximum_fusion.1), channel_id=1, source_target_pairs={{0,64},{32,96},{64,0},{96,32},{128,192},{160,224},{192,128},{224,1... | collective-permute-start | bytes 245768 | tf_op jit(solution)/shard_map/ppermute | solution.py:33
  34.0 2.7 %collective-permute-done.7.refs_3_ = f32[160,128]{1,0:T(8,128)S(1)} collective-permute-done((f32[160,128]{1,0:T(8,128)S(1)}, f32[160,128]{1,0:T(8,128)S(1)}, u32[]{:S(2)}, u32[]{:S(2)}) %collective-permute-start.7) | collective-permute-done | bytes 81952 | tf_op jit(solution)/shard_map/ppermute | solution.py:33
  36.7 2.8 %collective-permute-done.6.refs_2_ = f32[160,128]{1,0:T(8,128)S(1)} collective-permute-done((f32[160,128]{1,0:T(8,128)S(1)}, f32[160,128]{1,0:T(8,128)S(1)}, u32[]{:S(2)}, u32[]{:S(2)}) %collective-permute-start.6) | collective-permute-done | bytes 81952 | tf_op jit(solution)/shard_map/ppermute | solution.py:33
  39.5 0.0 collective-permute-done.5.refs_1_
  39.5 1.2 %smooth.1 = f32[640,128]{1,0:T(8,128)} custom-call(f32[32,32]{1,0:T(8,128)S(1)} %get-tuple-element.12.weights, f32[32,128]{1,0:T(8,128)S(1)} %get-tuple-element.13.totals, f32[160,128]{1,0:T(8,128)S(1)} %pad_maximum_fusion.refs_0_, f32[160,128]{1,0:T(8,128)S(1)} %collective-permute-done.5.refs_1_, f32[160,128]{1,0:T(8,128)S(1)} %collective-permute-done.6.refs_2_, ...), custom_call_target="tpu_custom_call" | custom-call | tf_op jit(solution)/shard_map/smooth/pallas_call | solution.py:212
  (22 shorter events, 0.3 us)
Async XLA Ops:
  0.0 8.8 %copy-start.1 = (bf16[1,5,128,12]{2,3,1,0:T(8,128)(2,1)S(1)}, bf16[1,5,128,12]{2,3,1,0:T(8,128)(2,1)}, u32[]{:S(2)}) copy-start(bf16[1,5,128,12]{2,3,1,0:T(8,128)(2,1)} %param.9) | copy-start | bytes 46084
  0.0 8.8 %copy-start.2 = (bf16[1,5,16,12]{3,2,1,0:T(8,128)(2,1)S(1)}, bf16[1,5,16,12]{3,2,1,0:T(8,128)(2,1)}, u32[]{:S(2)}) copy-start(bf16[1,5,16,12]{3,2,1,0:T(8,128)(2,1)} %refs_4_.3) | copy-start | bytes 5764
  0.0 8.8 %copy-start.5 = (s32[1,5]{1,0:T(1,128)S(1)}, s32[1,5]{1,0:T(1,128)}, u32[]{:S(2)}) copy-start(s32[1,5]{1,0:T(1,128)} %refs_1_.3) | copy-start | bytes 64
  0.0 8.8 %copy-start.6 = (s32[1,5]{1,0:T(1,128)S(1)}, s32[1,5]{1,0:T(1,128)}, u32[]{:S(2)}) copy-start(s32[1,5]{1,0:T(1,128)} %refs_2_.3) | copy-start | bytes 64
  0.0 8.8 %copy-start.4 = (s32[1,5]{1,0:T(1,128)S(1)}, s32[1,5]{1,0:T(1,128)}, u32[]{:S(2)}) copy-start(s32[1,5]{1,0:T(1,128)} %refs_0_.3) | copy-start | bytes 64
  0.0 8.8 %copy-start = (bf16[4,10,80,512]{3,2,1,0:T(8,128)(2,1)S(1)}, bf16[4,10,80,512]{3,2,1,0:T(8,128)(2,1)}, u32[]{:S(2)}) copy-start(bf16[4,10,80,512]{3,2,1,0:T(8,128)(2,1)} %refs_5_.3) | copy-start | bytes 9830404
  5.5 14.5 %copy-start.3 = (f32[32,32]{1,0:T(8,128)S(1)}, f32[32,32]{1,0:T(8,128)}, u32[]{:S(2)}) copy-start(f32[32,32]{1,0:T(8,128)} %smoother.1) | copy-start | bytes 12292
  5.6 14.5 %copy-start.7 = (s32[32,1]{0,1:T(1,128)S(1)}, s32[32,1]{0,1:T(1,128)}, u32[]{:S(2)}) copy-start(s32[32,1]{0,1:T(1,128)} %param.14) | copy-start | bytes 388
  5.6 9.7 %collective-permute-start = (f32[640,128]{1,0:T(8,128)}, f32[640,128]{1,0:T(8,128)S(1)}, u32[]{:S(2)}, u32[]{:S(2)}) collective-permute-start(f32[640,128]{1,0:T(8,128)} %get-tuple-element.16), channel_id=1, source_target_pairs={{0,1},{1,0},{2,3},{3,2},{4,5},{5,4},{6,7},{7,6},{8,9},{9,8},{10,11... | collective-permute-start | bytes 983048 | tf_op jit(solution)/shard_map/ppermute | solution.py:17
  7.1 12.7 %collective-permute-start.2 = (f32[640,128]{1,0:T(8,128)}, f32[640,128]{1,0:T(8,128)S(1)}, u32[]{:S(2)}, u32[]{:S(2)}) collective-permute-start(f32[640,128]{1,0:T(8,128)} %get-tuple-element.18), channel_id=1, source_target_pairs={{0,32},{1,2},{2,1},{3,4},{4,3},{5,6},{6,5},{7,8},{8,7},{9,10},{10,... | collective-permute-start | bytes 983048 | tf_op jit(solution)/shard_map/ppermute | solution.py:29
  15.4 12.0 %collective-permute-start.1 = (f32[640,128]{1,0:T(8,128)S(1)}, f32[640,128]{1,0:T(8,128)S(1)}, u32[]{:S(2)}, u32[]{:S(2)}) collective-permute-start(f32[640,128]{1,0:T(8,128)S(1)} %add.55), channel_id=1, source_target_pairs={{0,32},{1,2},{2,1},{3,4},{4,3},{5,6},{6,5},{7,8},{8,7},{9,10},{10,... | collective-permute-start | bytes 983048 | tf_op jit(solution)/shard_map/ppermute | solution.py:29
  19.9 8.4 %collective-permute-start.3 = (f32[640,128]{1,0:T(8,128)S(1)}, f32[640,128]{1,0:T(8,128)S(1)}, u32[]{:S(2)}, u32[]{:S(2)}) collective-permute-start(f32[640,128]{1,0:T(8,128)S(1)} %add.57), channel_id=1, source_target_pairs={{0,1},{1,0},{2,3},{3,2},{4,5},{5,4},{6,7},{7,6},{8,9},{9,8},{10,11... | collective-permute-start | bytes 983048 | tf_op jit(solution)/shard_map/ppermute | solution.py:17
  28.3 1.5 %collective-permute-start.4 = (f32[4,80,128]{2,1,0:T(8,128)S(1)}, f32[4,80,128]{2,1,0:T(8,128)S(1)}, u32[]{:S(2)}, u32[]{:S(2)}) collective-permute-start(f32[4,80,128]{2,1,0:T(8,128)S(1)} %fusion), channel_id=1, source_target_pairs={{0,32},{32,0},{64,96},{96,64},{128,160},{160,128},{192,224},{224,1... | collective-permute-start | bytes 491528 | tf_op jit(solution)/shard_map/ppermute | solution.py:33
  29.8 6.9 %collective-permute-start.7 = (f32[160,128]{1,0:T(8,128)S(1)}, f32[160,128]{1,0:T(8,128)S(1)}, u32[]{:S(2)}, u32[]{:S(2)}) collective-permute-start(f32[160,128]{1,0:T(8,128)S(1)} %pad_maximum_fusion.3), channel_id=1, source_target_pairs={{0,192},{32,224},{64,128},{96,160},{128,64},{160,96},{192,0},{224,... | collective-permute-start | bytes 245768 | tf_op jit(solution)/shard_map/ppermute | solution.py:33
  32.9 6.6 %collective-permute-start.6 = (f32[160,128]{1,0:T(8,128)S(1)}, f32[160,128]{1,0:T(8,128)S(1)}, u32[]{:S(2)}, u32[]{:S(2)}) collective-permute-start(f32[160,128]{1,0:T(8,128)S(1)} %pad_maximum_fusion.2), channel_id=1, source_target_pairs={{0,128},{32,160},{64,192},{96,224},{128,0},{160,32},{192,64},{224,... | collective-permute-start | bytes 245768 | tf_op jit(solution)/shard_map/ppermute | solution.py:33
  33.5 6.0 %collective-permute-start.5 = (f32[160,128]{1,0:T(8,128)S(1)}, f32[160,128]{1,0:T(8,128)S(1)}, u32[]{:S(2)}, u32[]{:S(2)}) collective-permute-start(f32[160,128]{1,0:T(8,128)S(1)} %pad_maximum_fusion.1), channel_id=1, source_target_pairs={{0,64},{32,96},{64,0},{96,32},{128,192},{160,224},{192,128},{224,1... | collective-permute-start | bytes 245768 | tf_op jit(solution)/shard_map/ppermute | solution.py:33

commit v4 on v3

v4 whole, which is shorter than its diff:
```python
import functools

import jax
import jax.numpy as jnp
from jax import lax
from jax.experimental import pallas as pl
from jax.experimental.pallas import tpu as pltpu
from jax.sharding import PartitionSpec as P

HIGHEST = lax.Precision.HIGHEST
LIMIT = 12 * 1024 * 1024


def even_swap(block):
    pairs = [(i, i ^ 1) for i in range(lax.axis_size("tile"))]
    return lax.ppermute(block, "tile", pairs)


def odd_swap(block):
    tiles = lax.axis_size("tile")
    pairs = []
    for date in range(lax.axis_size("date")):
        for tile in range(tiles):
            other, date_to = ((tile - 1) ^ 1) + 1, date
            if tile in (0, tiles - 1):
                other, date_to = tile, date ^ 1
            pairs.append((date * tiles + tile, date_to * tiles + other))
    return lax.ppermute(block, ("date", "tile"), pairs)


def date_swap(block, distance):
    return lax.ppermute(block, "date", [(i, i ^ distance) for i in range(lax.axis_size("date"))])


def resample_kernel(reaches, *refs):
    count = len(reaches)
    inputs, outs, scratch = refs[:6], refs[6 : 6 + count], refs[6 + count :]
    held, (x_mats, y_mats, sems, date_sems) = scratch[:6], scratch[6:]
    targets, row_offset, col_offset, coef_x, coef_y, granule = held
    slots, taps, tile_cols = coef_x.shape[1:]
    tile_rows = coef_y.shape[2]
    dates, bands, grid_rows, grid_cols = granule.shape

    small = [pltpu.make_async_copy(inputs[i], held[i], sems.at[i]) for i in range(5)]
    large = [
        pltpu.make_async_copy(inputs[5].at[d], granule.at[d], date_sems.at[d])
        for d in range(dates)
    ]
    for copy in small + large:
        copy.start()
    for copy in small + large[:2]:
        copy.wait()

    own = lax.axis_index("tile")
    side = 1 - 2 * lax.rem(own, 2)
    to_order = (
        lax.broadcasted_iota(jnp.int32, (tile_rows, tile_rows), 1)
        == 2 * lax.rem(lax.broadcasted_iota(jnp.int32, (tile_rows, tile_rows), 0), tile_rows // 2)
        + lax.broadcasted_iota(jnp.int32, (tile_rows, tile_rows), 0) // (tile_rows // 2)
    ).astype(jnp.float32)
    for n, reach in enumerate(reaches):
        wanted = own + side * reach
        slot = jnp.int32(0)
        used = jnp.int32(0)
        for k in range(slots):
            hit = jnp.logical_and(wanted >= 0, targets[0, k] == wanted).astype(jnp.int32)
            slot = slot + k * hit
            used = used + hit
        coeffs = jnp.pad(coef_x[0, slot].astype(jnp.float32), ((0, 16 - taps), (0, 0)))
        shift = (
            lax.broadcasted_iota(jnp.int32, (8, tile_cols), 0)
            - 2 * lax.broadcasted_iota(jnp.int32, (8, tile_cols), 1)
            - col_offset[0, slot]
        )
        for first in range(0, grid_cols, 16):
            halves = []
            for tap in (shift + first, shift + first + 8):
                place = tap & 7
                picked = jnp.where(
                    tap < 8,
                    jnp.take_along_axis(coeffs[:8], place, axis=0, mode="promise_in_bounds"),
                    jnp.take_along_axis(coeffs[8:], place, axis=0, mode="promise_in_bounds"),
                )
                halves.append(jnp.where((tap & ~15) == 0, picked, 0.0))
            x_mats[n, first : first + 16] = jnp.concatenate(halves, 0).astype(jnp.bfloat16)
        tap = (
            lax.broadcasted_iota(jnp.int32, (tile_rows, grid_rows), 1)
            - 2 * lax.broadcasted_iota(jnp.int32, (tile_rows, grid_rows), 0)
            - row_offset[0, slot]
        )
        tap = jnp.where(used > 0, tap, -1)
        coeffs = coef_y[0, slot].astype(jnp.float32)
        banded = jnp.zeros((tile_rows, grid_rows), jnp.float32)
        for t in range(taps):
            banded = jnp.where(tap == t, coeffs[:, t : t + 1], banded)
        ordered = jnp.dot(to_order, banded, preferred_element_type=jnp.float32)
        y_mats[n * tile_rows : (n + 1) * tile_rows] = ordered.astype(jnp.bfloat16)

    half = tile_rows // 2
    for date in range(dates):
        if date > 0 and date % 2 == 0:
            for copy in large[date : date + 2]:
                copy.wait()
        along_y = [
            jnp.dot(y_mats[...], granule[date, b], preferred_element_type=jnp.float32)
            for b in range(bands)
        ]
        for n in range(count):
            rows = jnp.concatenate([part[n * tile_rows : (n + 1) * tile_rows] for part in along_y], 0)
            high = rows.astype(jnp.bfloat16)
            low = (rows - high.astype(jnp.float32)).astype(jnp.bfloat16)
            partial = jnp.dot(high, x_mats[n], preferred_element_type=jnp.float32) + jnp.dot(
                low, x_mats[n], preferred_element_type=jnp.float32
            )
            stride = 2 * dates * bands
            for b in range(bands):
                for parity in range(2):
                    first = b * tile_rows + parity * half
                    at = date * 2 * bands + parity * bands + b
                    outs[n][pl.ds(at, half, stride=stride), :] = partial[first : first + half]


def resample(reaches, limit, targets, row_offset, col_offset, coef_x, coef_y, granules):
    dates, bands, grid_rows, grid_cols = granules.shape
    tile_cols = coef_x.shape[3]
    tile_rows = coef_y.shape[2]
    count = len(reaches)
    return pl.pallas_call(
        functools.partial(resample_kernel, reaches),
        in_specs=[pl.BlockSpec(memory_space=pltpu.HBM)] * 6,
        out_specs=[pl.BlockSpec(memory_space=pltpu.VMEM)] * count,
        out_shape=[jax.ShapeDtypeStruct((dates * bands * tile_rows, tile_cols), jnp.float32)] * count,
        scratch_shapes=[
            pltpu.SMEM(targets.shape, jnp.int32),
            pltpu.SMEM(row_offset.shape, jnp.int32),
            pltpu.SMEM(col_offset.shape, jnp.int32),
            pltpu.VMEM(coef_x.shape, coef_x.dtype),
            pltpu.VMEM(coef_y.shape, coef_y.dtype),
            pltpu.VMEM(granules.shape, granules.dtype),
            pltpu.VMEM((count, grid_cols, tile_cols), jnp.bfloat16),
            pltpu.VMEM((count * tile_rows, grid_rows), jnp.bfloat16),
            pltpu.SemaphoreType.DMA((5,)),
            pltpu.SemaphoreType.DMA((dates,)),
        ],
        compiler_params=pltpu.CompilerParams(vmem_limit_bytes=limit),
        cost_estimate=pl.CostEstimate(
            flops=count * dates * bands * tile_rows * grid_cols * (grid_rows + 4 * tile_cols),
            bytes_accessed=granules.size * 2,
            transcendentals=0,
        ),
        name="resample",
    )(targets, row_offset, col_offset, coef_x, coef_y, granules)


def weights_kernel(local_dates, mask, smoother, weights):
    dates = smoother.shape[0]
    masked = smoother[...] * mask[...].astype(jnp.float32)
    masked = masked / jnp.sum(masked, 1, keepdims=True)
    me = lax.axis_index("date")
    source = lax.broadcasted_iota(jnp.int32, (dates, dates), 0)
    place = lax.broadcasted_iota(jnp.int32, (dates, dates), 1)
    block = place // local_dates
    wanted = ((block ^ (2 * (block // 4))) ^ me) * local_dates + lax.rem(place, local_dates)
    picks = (source == wanted).astype(jnp.float32)
    ordered = jnp.dot(masked, picks, precision=HIGHEST, preferred_element_type=jnp.float32)
    high = ordered.astype(jnp.bfloat16).astype(jnp.float32)
    weights[...] = jnp.concatenate([high, high, ordered - high], 1)


def smoothing_weights(local_dates, mask, smoother):
    dates = smoother.shape[0]
    return pl.pallas_call(
        functools.partial(weights_kernel, local_dates),
        out_shape=jax.ShapeDtypeStruct((dates, 3 * dates), jnp.float32),
        compiler_params=pltpu.CompilerParams(vmem_limit_bytes=LIMIT),
        name="smoothing_weights",
    )(mask, smoother)


def smooth_kernel(weights, *refs):
    pieces, out = refs[:-1], refs[-1]
    dates, lanes = weights.shape[0], out.shape[1]
    rows = out.shape[0] // dates
    bands, held = rows // 2, dates // len(pieces)
    series = jnp.concatenate(
        [
            jnp.concatenate(
                [piece[pl.ds(parity * bands + b, held, stride=rows), :] for piece in pieces], 0
            )
            for b in range(bands)
            for parity in range(2)
        ],
        1,
    )
    high = series.astype(jnp.bfloat16)
    low = (series - high.astype(jnp.float32)).astype(jnp.bfloat16)
    total = jnp.dot(
        weights[...].astype(jnp.bfloat16),
        jnp.concatenate([high, low, high], 0),
        preferred_element_type=jnp.float32,
    )
    for row in range(rows):
        out[pl.ds(row, dates, stride=rows), :] = total[:, row * lanes : (row + 1) * lanes]


def smooth(weights, pieces):
    return pl.pallas_call(
        smooth_kernel,
        out_shape=jax.ShapeDtypeStruct(
            (sum(piece.shape[0] for piece in pieces), pieces[0].shape[1]), jnp.float32
        ),
        compiler_params=pltpu.CompilerParams(vmem_limit_bytes=LIMIT),
        name="smooth",
    )(weights, *pieces)


def to_pixel_blocks(terms):
    positions = lax.axis_size("date")
    me = lax.axis_index("date")
    core, y = lax.rem(me, 2), me // 2
    terms = [term.reshape(positions // 2, 2, -1, term.shape[-1]) for term in terms]

    def of_core(which):
        picked = [lax.dynamic_index_in_dim(term, which, 1, keepdims=False) for term in terms]
        return picked[0] + picked[1] + picked[2]

    mine, other = of_core(core), of_core(1 - core)
    got = date_swap(other, 1)
    blocks = []
    for distance in [i ^ (i // 2) for i in range(positions // 2)]:
        at = y ^ distance
        block = jnp.concatenate(
            [
                lax.dynamic_index_in_dim(mine, at, 0, keepdims=False),
                lax.dynamic_index_in_dim(got, at, 0, keepdims=False),
            ],
            0,
        )
        blocks.append(date_swap(block, 2 * distance) if distance else block)
    return blocks


def body(granules, coef_x, coef_y, row_offset, col_offset, targets, mask, smoother):
    local_dates, bands = granules.shape[:2]
    tile_cols = coef_x.shape[2]
    block_pix = tile_cols * coef_y.shape[2] // lax.axis_size("date")
    coef_x = jnp.transpose(coef_x, (0, 1, 3, 2))

    operands = (targets, row_offset, col_offset, coef_x, coef_y, granules)
    weights = smoothing_weights(local_dates, jnp.transpose(mask), smoother)
    far_even, far_odd = resample((2, -2), 56 * 1024 * 1024, *operands)
    from_odd = odd_swap(far_odd)
    from_even = even_swap(far_even)
    even, odd, own = resample((1, -1, 0), LIMIT, *operands)
    arrived_odd = odd_swap(odd + from_even)
    arrived_even = even_swap(even + from_odd)
    blocks = to_pixel_blocks((own, arrived_odd, arrived_even))
    smoothed = smooth(weights, blocks)
    return smoothed.reshape(smoother.shape[0], bands, 1, block_pix)


def solution(mesh):
    return jax.shard_map(
        body,
        mesh=mesh,
        in_specs=(
            P("date", None, "tile", None),
            P("tile", None, None, None),
            P("tile", None, None, None),
            P("tile", None),
            P("tile", None),
            P("tile", None),
            P(None, "tile"),
            P(),
        ),
        out_specs=P(None, None, "tile", "date"),
        check_vma=False,
    )
```

time: 40.8 us -> 38.9 us (0.953)
  Pallas kernels: 11.4 us -> 9.27 us
    pallas_call x3, Pallas kernels: 11.2 us -> 8.98 us  [the longest x2 8.05 us: resample(): pl.pallas_call(functools.partial(resample_kernel, reaches), in_specs=[pl....]
    ppermute x2, waiting for transfers between devices: 2.87 us -> 4.07 us  [even_swap(): return lax.ppermute(block, 'tile', pairs)]
    ppermute x4, waiting for transfers between devices: 6.78 us -> 5.85 us  [date_swap(): lax.ppermute(block, 'date', [(i, i ^ distance) for i in range(lax.axis_si...]
  transfers between devices with their start and end apart: 8 -> 8, of which waited for: 7 -> 7; matrix products, arithmetic and copies ran while one was open for 0% -> 0% of each run, Pallas kernels for 11% -> 9%
where the time goes in v4:
time: 38.9 us
  waiting for transfers between devices  19 us (49%)
  starting transfers between devices  10.1 us (26%)
  Pallas kernels  9.27 us (24%)
    ppermute x2, waiting for transfers between devices, odd_swap(): return lax.ppermute(block, ('date', 'tile'), pairs)  9.11 us
    pallas_call x2, Pallas kernels, resample(): pl.pallas_call(functools.partial(resample_kernel, reaches), in_specs=[pl....  8.05 us
    ppermute x4, waiting for transfers between devices, date_swap(): lax.ppermute(block, 'date', [(i, i ^ distance) for i in range(lax.axis_si...  5.85 us
    ppermute x4, starting transfers between devices, date_swap(): lax.ppermute(block, 'date', [(i, i ^ distance) for i in range(lax.axis_si...  4.43 us
    ppermute x2, waiting for transfers between devices, even_swap(): return lax.ppermute(block, 'tile', pairs)  4.07 us
    ppermute x2, starting transfers between devices, odd_swap(): return lax.ppermute(block, ('date', 'tile'), pairs)  4.01 us
    ppermute x2, starting transfers between devices, even_swap(): return lax.ppermute(block, 'tile', pairs)  1.66 us
    pallas_call x1, Pallas kernels, smooth(): pl.pallas_call(smooth_kernel, out_shape=jax.ShapeDtypeStruct((sum((piece....  0.93 us
  transfers between devices with their start and end apart: 8, of which 7 were waited for; matrix products, arithmetic and copies ran while one was open for 0% of the time, Pallas kernels for 9%

profile of v4, /device:TPU:128, one launch (start us, length us, event | category | flops | bytes accessed | tf_op | source)
XLA Modules:
  0.0 38.9 jit_solution(17918556223084620133)
XLA Ops:
  0.0 0.0 copy-start.6
  0.0 4.7 %resample.3 = (f32[640,128]{1,0:T(8,128)}, f32[640,128]{1,0:T(8,128)}) custom-call(s32[1,5]{1,0:T(1,128)} %refs_0_.3, s32[1,5]{1,0:T(1,128)} %refs_1_.3, s32[1,5]{1,0:T(1,128)} %refs_2_.3, bf16[1,5,12,128]{3,2,1,0:T(8,128)(2,1)} %bitcast.36, bf16[1,5,16,12]{3,2,1,0:T(8,128)(2,1)} %refs_4_.3, bf16[4,10,80,512]{3,2,1,0:T(8,128)(2,1)} %refs_5_.3), custom_call_target="tpu_custom_call" | custom-call | flops 387973120 | bytes 3276800 | tf_op jit(solution)/shard_map/resample/pallas_call | solution.py:128
  4.8 0.0 copy-start.3
  4.8 0.0 copy-start.7
  4.8 1.6 %collective-permute-start = (f32[640,128]{1,0:T(8,128)}, f32[640,128]{1,0:T(8,128)S(1)}, u32[]{:S(2)}, u32[]{:S(2)}) collective-permute-start(f32[640,128]{1,0:T(8,128)} %get-tuple-element.12), channel_id=1, source_target_pairs={{0,1},{1,0},{2,3},{3,2},{4,5},{5,4},{6,7},{7,6},{8,9},{9,8},{10,11... | collective-permute-start | bytes 983048 | tf_op jit(solution)/shard_map/ppermute | solution.py:16
  6.4 1.6 %collective-permute-start.2 = (f32[640,128]{1,0:T(8,128)}, f32[640,128]{1,0:T(8,128)S(1)}, u32[]{:S(2)}, u32[]{:S(2)}) collective-permute-start(f32[640,128]{1,0:T(8,128)} %get-tuple-element.14), channel_id=1, source_target_pairs={{0,32},{1,2},{2,1},{3,4},{4,3},{5,6},{6,5},{7,8},{8,7},{9,10},{10,... | collective-permute-start | bytes 983048 | tf_op jit(solution)/shard_map/ppermute | solution.py:28
  8.0 0.0 copy-done.6
  8.0 3.3 %resample.2 = (f32[640,128]{1,0:T(8,128)S(1)}, f32[640,128]{1,0:T(8,128)S(1)}, f32[640,128]{1,0:T(8,128)S(1)}) custom-call(s32[1,5]{1,0:T(1,128)S(1)} %copy-done.4, s32[1,5]{1,0:T(1,128)S(1)} %copy-done.5, s32[1,5]{1,0:T(1,128)S(1)} %copy-done.6, bf16[1,5,12,128]{3,2,1,0:T(8,128)(2,1)S(1)} %bitcast.37, bf16[1,5,16,12]{3,2,1,0:T(8,128)(2,1)S(1)} %copy-done.2, ...), custom_call_target="tpu_custom_call" | custom-call | flops 581959680 | bytes 3276800 | tf_op jit(solution)/shard_map/resample/pallas_call | solution.py:128
  11.4 3.2 %collective-permute-done = f32[640,128]{1,0:T(8,128)S(1)} collective-permute-done((f32[640,128]{1,0:T(8,128)}, f32[640,128]{1,0:T(8,128)S(1)}, u32[]{:S(2)}, u32[]{:S(2)}) %collective-permute-start) | collective-permute-done | bytes 327712 | tf_op jit(solution)/shard_map/ppermute | solution.py:16
  14.6 2.4 %collective-permute-start.1 = (f32[640,128]{1,0:T(8,128)S(1)}, f32[640,128]{1,0:T(8,128)S(1)}, u32[]{:S(2)}, u32[]{:S(2)}) collective-permute-start(f32[640,128]{1,0:T(8,128)S(1)} %add.55), channel_id=1, source_target_pairs={{0,32},{1,2},{2,1},{3,4},{4,3},{5,6},{6,5},{7,8},{8,7},{9,10},{10,... | collective-permute-start | bytes 983048 | tf_op jit(solution)/shard_map/ppermute | solution.py:28
  17.0 2.1 %collective-permute-done.2 = f32[640,128]{1,0:T(8,128)S(1)} collective-permute-done((f32[640,128]{1,0:T(8,128)}, f32[640,128]{1,0:T(8,128)S(1)}, u32[]{:S(2)}, u32[]{:S(2)}) %collective-permute-start.2) | collective-permute-done | bytes 327712 | tf_op jit(solution)/shard_map/ppermute | solution.py:28
  19.1 0.1 collective-permute-start.3
  19.3 0.3 smoothing_weights.1.weights
  19.6 7.0 %collective-permute-done.1 = f32[640,128]{1,0:T(8,128)S(1)} collective-permute-done((f32[640,128]{1,0:T(8,128)S(1)}, f32[640,128]{1,0:T(8,128)S(1)}, u32[]{:S(2)}, u32[]{:S(2)}) %collective-permute-start.1) | collective-permute-done | bytes 327712 | tf_op jit(solution)/shard_map/ppermute | solution.py:28
  26.6 0.9 %collective-permute-done.3 = f32[640,128]{1,0:T(8,128)S(1)} collective-permute-done((f32[640,128]{1,0:T(8,128)S(1)}, f32[640,128]{1,0:T(8,128)S(1)}, u32[]{:S(2)}, u32[]{:S(2)}) %collective-permute-start.3) | collective-permute-done | bytes 327712 | tf_op jit(solution)/shard_map/ppermute | solution.py:16
  27.5 0.1 collective-permute-start.4
  27.7 1.3 %collective-permute-done.4 = f32[4,80,128]{2,1,0:T(8,128)S(1)} collective-permute-done((f32[4,80,128]{2,1,0:T(8,128)S(1)}, f32[4,80,128]{2,1,0:T(8,128)S(1)}, u32[]{:S(2)}, u32[]{:S(2)}) %collective-permute-start.4) | collective-permute-done | bytes 163872 | tf_op jit(solution)/shard_map/ppermute | solution.py:32
  29.0 3.3 %collective-permute-start.7 = (f32[160,128]{1,0:T(8,128)S(1)}, f32[160,128]{1,0:T(8,128)S(1)}, u32[]{:S(2)}, u32[]{:S(2)}) collective-permute-start(f32[160,128]{1,0:T(8,128)S(1)} %pad_maximum_fusion.3), channel_id=1, source_target_pairs={{0,128},{32,160},{64,192},{96,224},{128,0},{160,32},{192,64},{224,... | collective-permute-start | bytes 245768 | tf_op jit(solution)/shard_map/ppermute | solution.py:32
  32.3 1.1 %collective-permute-start.6 = (f32[160,128]{1,0:T(8,128)S(1)}, f32[160,128]{1,0:T(8,128)S(1)}, u32[]{:S(2)}, u32[]{:S(2)}) collective-permute-start(f32[160,128]{1,0:T(8,128)S(1)} %pad_maximum_fusion.2), channel_id=1, source_target_pairs={{0,192},{32,224},{64,128},{96,160},{128,64},{160,96},{192,0},{224,... | collective-permute-start | bytes 245768 | tf_op jit(solution)/shard_map/ppermute | solution.py:32
  33.4 0.0 collective-permute-start.5
  33.4 1.7 %collective-permute-done.7.refs_3_ = f32[160,128]{1,0:T(8,128)S(1)} collective-permute-done((f32[160,128]{1,0:T(8,128)S(1)}, f32[160,128]{1,0:T(8,128)S(1)}, u32[]{:S(2)}, u32[]{:S(2)}) %collective-permute-start.7) | collective-permute-done | bytes 81952 | tf_op jit(solution)/shard_map/ppermute | solution.py:32
  35.1 2.8 %collective-permute-done.6.refs_2_ = f32[160,128]{1,0:T(8,128)S(1)} collective-permute-done((f32[160,128]{1,0:T(8,128)S(1)}, f32[160,128]{1,0:T(8,128)S(1)}, u32[]{:S(2)}, u32[]{:S(2)}) %collective-permute-start.6) | collective-permute-done | bytes 81952 | tf_op jit(solution)/shard_map/ppermute | solution.py:32
  38.0 0.0 collective-permute-done.5.refs_1_
  38.0 0.9 %smooth.1 = f32[640,128]{1,0:T(8,128)} custom-call(f32[32,96]{1,0:T(8,128)S(1)} %smoothing_weights.1.weights, f32[160,128]{1,0:T(8,128)S(1)} %pad_maximum_fusion.refs_0_, f32[160,128]{1,0:T(8,128)S(1)} %collective-permute-done.5.refs_1_, f32[160,128]{1,0:T(8,128)S(1)} %collective-permute-done.6.refs_2_, f32[160,128]{1,0:T(8,128)S(1)} %collective-permute-done.7.refs_3_), custom_call_target="tpu_custom_call" | custom-call | tf_op jit(solution)/shard_map/smooth/pallas_call | solution.py:207
  (22 shorter events, 0.3 us)
Async XLA Ops:
  0.0 8.0 %copy-start.1 = (bf16[1,5,128,12]{2,3,1,0:T(8,128)(2,1)S(1)}, bf16[1,5,128,12]{2,3,1,0:T(8,128)(2,1)}, u32[]{:S(2)}) copy-start(bf16[1,5,128,12]{2,3,1,0:T(8,128)(2,1)} %param.9) | copy-start | bytes 46084
  0.0 8.0 %copy-start.2 = (bf16[1,5,16,12]{3,2,1,0:T(8,128)(2,1)S(1)}, bf16[1,5,16,12]{3,2,1,0:T(8,128)(2,1)}, u32[]{:S(2)}) copy-start(bf16[1,5,16,12]{3,2,1,0:T(8,128)(2,1)} %refs_4_.3) | copy-start | bytes 5764
  0.0 8.0 %copy-start.5 = (s32[1,5]{1,0:T(1,128)S(1)}, s32[1,5]{1,0:T(1,128)}, u32[]{:S(2)}) copy-start(s32[1,5]{1,0:T(1,128)} %refs_1_.3) | copy-start | bytes 64
  0.0 8.0 %copy-start.6 = (s32[1,5]{1,0:T(1,128)S(1)}, s32[1,5]{1,0:T(1,128)}, u32[]{:S(2)}) copy-start(s32[1,5]{1,0:T(1,128)} %refs_2_.3) | copy-start | bytes 64
  0.0 8.0 %copy-start.4 = (s32[1,5]{1,0:T(1,128)S(1)}, s32[1,5]{1,0:T(1,128)}, u32[]{:S(2)}) copy-start(s32[1,5]{1,0:T(1,128)} %refs_0_.3) | copy-start | bytes 64
  0.0 8.0 %copy-start = (bf16[4,10,80,512]{3,2,1,0:T(8,128)(2,1)S(1)}, bf16[4,10,80,512]{3,2,1,0:T(8,128)(2,1)}, u32[]{:S(2)}) copy-start(bf16[4,10,80,512]{3,2,1,0:T(8,128)(2,1)} %refs_5_.3) | copy-start | bytes 9830404
  4.8 14.5 %copy-start.3 = (f32[32,32]{1,0:T(8,128)S(1)}, f32[32,32]{1,0:T(8,128)}, u32[]{:S(2)}) copy-start(f32[32,32]{1,0:T(8,128)} %smoother.1) | copy-start | bytes 12292
  4.8 14.5 %copy-start.7 = (s32[32,1]{0,1:T(1,128)S(1)}, s32[32,1]{0,1:T(1,128)}, u32[]{:S(2)}) copy-start(s32[32,1]{0,1:T(1,128)} %param.14) | copy-start | bytes 388
  4.8 9.7 %collective-permute-start = (f32[640,128]{1,0:T(8,128)}, f32[640,128]{1,0:T(8,128)S(1)}, u32[]{:S(2)}, u32[]{:S(2)}) collective-permute-start(f32[640,128]{1,0:T(8,128)} %get-tuple-element.12), channel_id=1, source_target_pairs={{0,1},{1,0},{2,3},{3,2},{4,5},{5,4},{6,7},{7,6},{8,9},{9,8},{10,11... | collective-permute-start | bytes 983048 | tf_op jit(solution)/shard_map/ppermute | solution.py:16
  6.4 12.7 %collective-permute-start.2 = (f32[640,128]{1,0:T(8,128)}, f32[640,128]{1,0:T(8,128)S(1)}, u32[]{:S(2)}, u32[]{:S(2)}) collective-permute-start(f32[640,128]{1,0:T(8,128)} %get-tuple-element.14), channel_id=1, source_target_pairs={{0,32},{1,2},{2,1},{3,4},{4,3},{5,6},{6,5},{7,8},{8,7},{9,10},{10,... | collective-permute-start | bytes 983048 | tf_op jit(solution)/shard_map/ppermute | solution.py:28
  14.6 12.0 %collective-permute-start.1 = (f32[640,128]{1,0:T(8,128)S(1)}, f32[640,128]{1,0:T(8,128)S(1)}, u32[]{:S(2)}, u32[]{:S(2)}) collective-permute-start(f32[640,128]{1,0:T(8,128)S(1)} %add.55), channel_id=1, source_target_pairs={{0,32},{1,2},{2,1},{3,4},{4,3},{5,6},{6,5},{7,8},{8,7},{9,10},{10,... | collective-permute-start | bytes 983048 | tf_op jit(solution)/shard_map/ppermute | solution.py:28
  19.1 8.4 %collective-permute-start.3 = (f32[640,128]{1,0:T(8,128)S(1)}, f32[640,128]{1,0:T(8,128)S(1)}, u32[]{:S(2)}, u32[]{:S(2)}) collective-permute-start(f32[640,128]{1,0:T(8,128)S(1)} %add.57), channel_id=1, source_target_pairs={{0,1},{1,0},{2,3},{3,2},{4,5},{5,4},{6,7},{7,6},{8,9},{9,8},{10,11... | collective-permute-start | bytes 983048 | tf_op jit(solution)/shard_map/ppermute | solution.py:16
  27.5 1.5 %collective-permute-start.4 = (f32[4,80,128]{2,1,0:T(8,128)S(1)}, f32[4,80,128]{2,1,0:T(8,128)S(1)}, u32[]{:S(2)}, u32[]{:S(2)}) collective-permute-start(f32[4,80,128]{2,1,0:T(8,128)S(1)} %fusion), channel_id=1, source_target_pairs={{0,32},{32,0},{64,96},{96,64},{128,160},{160,128},{192,224},{224,1... | collective-permute-start | bytes 491528 | tf_op jit(solution)/shard_map/ppermute | solution.py:32
  29.0 6.1 %collective-permute-start.7 = (f32[160,128]{1,0:T(8,128)S(1)}, f32[160,128]{1,0:T(8,128)S(1)}, u32[]{:S(2)}, u32[]{:S(2)}) collective-permute-start(f32[160,128]{1,0:T(8,128)S(1)} %pad_maximum_fusion.3), channel_id=1, source_target_pairs={{0,128},{32,160},{64,192},{96,224},{128,0},{160,32},{192,64},{224,... | collective-permute-start | bytes 245768 | tf_op jit(solution)/shard_map/ppermute | solution.py:32
  32.3 5.7 %collective-permute-start.6 = (f32[160,128]{1,0:T(8,128)S(1)}, f32[160,128]{1,0:T(8,128)S(1)}, u32[]{:S(2)}, u32[]{:S(2)}) collective-permute-start(f32[160,128]{1,0:T(8,128)S(1)} %pad_maximum_fusion.2), channel_id=1, source_target_pairs={{0,192},{32,224},{64,128},{96,160},{128,64},{160,96},{192,0},{224,... | collective-permute-start | bytes 245768 | tf_op jit(solution)/shard_map/ppermute | solution.py:32
  33.4 4.6 %collective-permute-start.5 = (f32[160,128]{1,0:T(8,128)S(1)}, f32[160,128]{1,0:T(8,128)S(1)}, u32[]{:S(2)}, u32[]{:S(2)}) collective-permute-start(f32[160,128]{1,0:T(8,128)S(1)} %pad_maximum_fusion.1), channel_id=1, source_target_pairs={{0,64},{32,96},{64,0},{96,32},{128,192},{160,224},{192,128},{224,1... | collective-permute-start | bytes 245768 | tf_op jit(solution)/shard_map/ppermute | solution.py:32

commit v5 on v4

--- a/solution.py
+++ b/solution.py
@@ -11,21 +11,23 @@
 LIMIT = 12 * 1024 * 1024
 
 
-def even_swap(block):
-    pairs = [(i, i ^ 1) for i in range(lax.axis_size("tile"))]
-    return lax.ppermute(block, "tile", pairs)
-
-
-def odd_swap(block):
+def joint_swap(block, partner, flip):
     tiles = lax.axis_size("tile")
     pairs = []
     for date in range(lax.axis_size("date")):
         for tile in range(tiles):
-            other, date_to = ((tile - 1) ^ 1) + 1, date
-            if tile in (0, tiles - 1):
-                other, date_to = tile, date ^ 1
-            pairs.append((date * tiles + tile, date_to * tiles + other))
+            to = partner(tile)
+            to_date = date ^ flip if 0 <= to < tiles else date ^ 1
+            pairs.append((date * tiles + tile, to_date * tiles + (to if 0 <= to < tiles else tile)))
     return lax.ppermute(block, ("date", "tile"), pairs)
+
+
+def even_swap(block, flip=0):
+    return joint_swap(block, lambda tile: tile ^ 1, flip)
+
+
+def odd_swap(block, flip=0):
+    return joint_swap(block, lambda tile: ((tile - 1) ^ 1) + 1, flip)
 
 
 def date_swap(block, distance):
@@ -53,10 +55,13 @@
 
     own = lax.axis_index("tile")
     side = 1 - 2 * lax.rem(own, 2)
+    core = lax.rem(lax.axis_index("date"), 2)
+    half = tile_rows // 2
+    row = lax.broadcasted_iota(jnp.int32, (tile_rows, tile_rows), 0)
+    place = lax.rem(row, half)
+    block = 2 * lax.rem(place, half // 2) + (place // (half // 2) ^ core)
     to_order = (
-        lax.broadcasted_iota(jnp.int32, (tile_rows, tile_rows), 1)
-        == 2 * lax.rem(lax.broadcasted_iota(jnp.int32, (tile_rows, tile_rows), 0), tile_rows // 2)
-        + lax.broadcasted_iota(jnp.int32, (tile_rows, tile_rows), 0) // (tile_rows // 2)
+        lax.broadcasted_iota(jnp.int32, (tile_rows, tile_rows), 1) == 2 * block + row // half
     ).astype(jnp.float32)
     for n, reach in enumerate(reaches):
         wanted = own + side * reach
@@ -96,7 +101,6 @@
         ordered = jnp.dot(to_order, banded, preferred_element_type=jnp.float32)
         y_mats[n * tile_rows : (n + 1) * tile_rows] = ordered.astype(jnp.bfloat16)
 
-    half = tile_rows // 2
     for date in range(dates):
         if date > 0 and date % 2 == 0:
             for copy in large[date : date + 2]:
@@ -214,18 +218,10 @@
     )(weights, *pieces)
 
 
-def to_pixel_blocks(terms):
+def to_pixel_blocks(mine, got):
     positions = lax.axis_size("date")
-    me = lax.axis_index("date")
-    core, y = lax.rem(me, 2), me // 2
-    terms = [term.reshape(positions // 2, 2, -1, term.shape[-1]) for term in terms]
-
-    def of_core(which):
-        picked = [lax.dynamic_index_in_dim(term, which, 1, keepdims=False) for term in terms]
-        return picked[0] + picked[1] + picked[2]
-
-    mine, other = of_core(core), of_core(1 - core)
-    got = date_swap(other, 1)
+    y = lax.axis_index("date") // 2
+    mine, got = [part.reshape(positions // 2, -1, part.shape[-1]) for part in (mine, got)]
     blocks = []
     for distance in [i ^ (i // 2) for i in range(positions // 2)]:
         at = y ^ distance
@@ -252,9 +248,14 @@
     from_odd = odd_swap(far_odd)
     from_even = even_swap(far_even)
     even, odd, own = resample((1, -1, 0), LIMIT, *operands)
-    arrived_odd = odd_swap(odd + from_even)
-    arrived_even = even_swap(even + from_odd)
-    blocks = to_pixel_blocks((own, arrived_odd, arrived_even))
+    half = own.shape[0] // 2
+    mine, other = slice(0, half), slice(half, None)
+    odd_mine = odd_swap(odd[mine] + from_even[mine])
+    odd_got = odd_swap(odd[other] + from_even[other], 1)
+    even_mine = even_swap(even[mine] + from_odd[mine])
+    even_got = even_swap(even[other] + from_odd[other], 1)
+    own_got = date_swap(own[other], 1)
+    blocks = to_pixel_blocks(own[mine] + odd_mine + even_mine, own_got + odd_got + even_got)
     smoothed = smooth(weights, blocks)
     return smoothed.reshape(smoother.shape[0], bands, 1, block_pix)
 

time: 38.9 us -> 38 us (0.977)
  waiting for transfers between devices: 19 us -> 16 us
  starting transfers between devices: 10.1 us -> 12.2 us
    ppermute x4 -> x6, starting transfers between devices: 5.67 us -> 7.77 us  [joint_swap(): return lax.ppermute(block, ('date', 'tile'), pairs)]
    ppermute x4 -> x6, waiting for transfers between devices: 13.2 us -> 11.4 us  [joint_swap(): return lax.ppermute(block, ('date', 'tile'), pairs)]
    ppermute x4, waiting for transfers between devices: 5.85 us -> 4.58 us  [date_swap(): lax.ppermute(block, 'date', [(i, i ^ distance) for i in range(lax.axis_si...]
  transfers between devices with their start and end apart: 8 -> 10, of which waited for: 7 -> 7; matrix products, arithmetic and copies ran while one was open for 0% -> 0% of each run, Pallas kernels for 9% -> 10%
where the time goes in v5:
time: 38 us; the launch traced here: 37.9 us
  waiting for transfers between devices  16 us (42%)
  starting transfers between devices  12.2 us (32%)
  Pallas kernels  9.24 us (24%)
    ppermute x6, waiting for transfers between devices, joint_swap(): return lax.ppermute(block, ('date', 'tile'), pairs)  11.4 us
    pallas_call x2, Pallas kernels, resample(): pl.pallas_call(functools.partial(resample_kernel, reaches), in_specs=[pl....  8.02 us
    ppermute x6, starting transfers between devices, joint_swap(): return lax.ppermute(block, ('date', 'tile'), pairs)  7.77 us
    ppermute x4, waiting for transfers between devices, date_swap(): lax.ppermute(block, 'date', [(i, i ^ distance) for i in range(lax.axis_si...  4.58 us
    ppermute x4, starting transfers between devices, date_swap(): lax.ppermute(block, 'date', [(i, i ^ distance) for i in range(lax.axis_si...  4.44 us
    pallas_call x1, Pallas kernels, smooth(): pl.pallas_call(smooth_kernel, out_shape=jax.ShapeDtypeStruct((sum((piece....  0.93 us
  transfers between devices with their start and end apart: 10, of which 7 were waited for; matrix products, arithmetic and copies ran while one was open for 0% of the time, Pallas kernels for 10%

profile of v5, /device:TPU:128, one launch (start us, length us, event | category | flops | bytes accessed | tf_op | source)
XLA Modules:
  0.0 37.9 jit_solution(32739502045370248)
XLA Ops:
  0.0 4.7 %resample.3 = (f32[640,128]{1,0:T(8,128)}, f32[640,128]{1,0:T(8,128)}) custom-call(s32[1,5]{1,0:T(1,128)} %refs_0_.3, s32[1,5]{1,0:T(1,128)} %refs_1_.3, s32[1,5]{1,0:T(1,128)} %refs_2_.3, bf16[1,5,12,128]{3,2,1,0:T(8,128)(2,1)} %bitcast.21, bf16[1,5,16,12]{3,2,1,0:T(8,128)(2,1)} %refs_4_.3, bf16[4,10,80,512]{3,2,1,0:T(8,128)(2,1)} %refs_5_.3), custom_call_target="tpu_custom_call" | custom-call | flops 387973120 | bytes 3276800 | tf_op jit(solution)/shard_map/resample/pallas_call | solution.py:132
  4.7 0.0 copy-start.3
  4.7 0.0 copy-start.7
  4.8 1.6 %collective-permute-start = (f32[640,128]{1,0:T(8,128)}, f32[640,128]{1,0:T(8,128)S(1)}, u32[]{:S(2)}, u32[]{:S(2)}) collective-permute-start(f32[640,128]{1,0:T(8,128)} %get-tuple-element.12), channel_id=1, source_target_pairs={{0,1},{1,0},{2,3},{3,2},{4,5},{5,4},{6,7},{7,6},{8,9},{9,8},{10,11... | collective-permute-start | bytes 983048 | tf_op jit(solution)/shard_map/ppermute | solution.py:22
  6.3 1.6 %collective-permute-start.2 = (f32[640,128]{1,0:T(8,128)}, f32[640,128]{1,0:T(8,128)S(1)}, u32[]{:S(2)}, u32[]{:S(2)}) collective-permute-start(f32[640,128]{1,0:T(8,128)} %get-tuple-element.14), channel_id=1, source_target_pairs={{0,32},{1,2},{2,1},{3,4},{4,3},{5,6},{6,5},{7,8},{8,7},{9,10},{10,... | collective-permute-start | bytes 983048 | tf_op jit(solution)/shard_map/ppermute | solution.py:22
  8.0 3.3 %resample.2 = (f32[640,128]{1,0:T(8,128)S(1)}, f32[640,128]{1,0:T(8,128)S(1)}, f32[640,128]{1,0:T(8,128)S(1)}) custom-call(s32[1,5]{1,0:T(1,128)S(1)} %copy-done.4, s32[1,5]{1,0:T(1,128)S(1)} %copy-done.5, s32[1,5]{1,0:T(1,128)S(1)} %copy-done.6, bf16[1,5,12,128]{3,2,1,0:T(8,128)(2,1)S(1)} %bitcast.22, bf16[1,5,16,12]{3,2,1,0:T(8,128)(2,1)S(1)} %copy-done.2, ...), custom_call_target="tpu_custom_call" | custom-call | flops 581959680 | bytes 3276800 | tf_op jit(solution)/shard_map/resample/pallas_call | solution.py:132
  11.4 3.1 %collective-permute-done = f32[640,128]{1,0:T(8,128)S(1)} collective-permute-done((f32[640,128]{1,0:T(8,128)}, f32[640,128]{1,0:T(8,128)S(1)}, u32[]{:S(2)}, u32[]{:S(2)}) %collective-permute-start) | collective-permute-done | bytes 327712 | tf_op jit(solution)/shard_map/ppermute | solution.py:22
  14.5 2.4 %collective-permute-start.1 = (f32[320,128]{1,0:T(8,128)S(1)}, f32[320,128]{1,0:T(8,128)S(1)}, u32[]{:S(2)}, u32[]{:S(2)}) collective-permute-start(f32[320,128]{1,0:T(8,128)S(1)} %get-tuple-element.15), channel_id=1, source_target_pairs={{0,32},{1,2},{2,1},{3,4},{4,3},{5,6},{6,5},{7,8},{8,7},{9,10},{10,... | collective-permute-start | bytes 491528 | tf_op jit(solution)/shard_map/ppermute | solution.py:22
  16.9 2.1 %collective-permute-done.2 = f32[640,128]{1,0:T(8,128)S(1)} collective-permute-done((f32[640,128]{1,0:T(8,128)}, f32[640,128]{1,0:T(8,128)S(1)}, u32[]{:S(2)}, u32[]{:S(2)}) %collective-permute-start.2) | collective-permute-done | bytes 327712 | tf_op jit(solution)/shard_map/ppermute | solution.py:22
  19.1 0.1 collective-permute-start.3
  19.2 0.1 collective-permute-start.5
  19.3 1.9 %collective-permute-start.6 = (f32[320,128]{1,0:T(8,128)S(1)}, f32[320,128]{1,0:T(8,128)S(1)}, u32[]{:S(2)}, u32[]{:S(2)}) collective-permute-start(f32[320,128]{1,0:T(8,128)S(1)} %get-tuple-element.18), channel_id=1, source_target_pairs={{0,33},{1,32},{2,35},{3,34},{4,37},{5,36},{6,39},{7,38},{8,41},{9,... | collective-permute-start | bytes 491528 | tf_op jit(solution)/shard_map/ppermute | solution.py:22
  21.2 2.0 %collective-permute-done.1 = f32[320,128]{1,0:T(8,128)S(1)} collective-permute-done((f32[320,128]{1,0:T(8,128)S(1)}, f32[320,128]{1,0:T(8,128)S(1)}, u32[]{:S(2)}, u32[]{:S(2)}) %collective-permute-start.1) | collective-permute-done | bytes 163872 | tf_op jit(solution)/shard_map/ppermute | solution.py:22
  23.3 2.7 %collective-permute-done.3 = f32[320,128]{1,0:T(8,128)S(1)} collective-permute-done((f32[320,128]{1,0:T(8,128)S(1)}, f32[320,128]{1,0:T(8,128)S(1)}, u32[]{:S(2)}, u32[]{:S(2)}) %collective-permute-start.3) | collective-permute-done | bytes 163872 | tf_op jit(solution)/shard_map/ppermute | solution.py:22
  26.0 0.1 collective-permute-start.4
  26.2 0.3 smoothing_weights.1.weights
  26.4 1.4 %collective-permute-done.5 = f32[320,128]{1,0:T(8,128)S(1)} collective-permute-done((f32[320,128]{1,0:T(8,128)S(1)}, f32[320,128]{1,0:T(8,128)S(1)}, u32[]{:S(2)}, u32[]{:S(2)}) %collective-permute-start.5) | collective-permute-done | bytes 163872 | tf_op jit(solution)/shard_map/ppermute | solution.py:22
  27.9 0.0 collective-permute-done.6
  27.9 0.0 collective-permute-done.4
  28.0 3.3 %collective-permute-start.9 = (f32[160,128]{1,0:T(8,128)S(1)}, f32[160,128]{1,0:T(8,128)S(1)}, u32[]{:S(2)}, u32[]{:S(2)}) collective-permute-start(f32[160,128]{1,0:T(8,128)S(1)} %pad_maximum_fusion.3), channel_id=1, source_target_pairs={{0,128},{32,160},{64,192},{96,224},{128,0},{160,32},{192,64},{224,... | collective-permute-start | bytes 245768 | tf_op jit(solution)/shard_map/ppermute | solution.py:34
  31.3 1.0 %collective-permute-start.8 = (f32[160,128]{1,0:T(8,128)S(1)}, f32[160,128]{1,0:T(8,128)S(1)}, u32[]{:S(2)}, u32[]{:S(2)}) collective-permute-start(f32[160,128]{1,0:T(8,128)S(1)} %pad_maximum_fusion.2), channel_id=1, source_target_pairs={{0,192},{32,224},{64,128},{96,160},{128,64},{160,96},{192,0},{224,... | collective-permute-start | bytes 245768 | tf_op jit(solution)/shard_map/ppermute | solution.py:34
  32.4 1.6 %collective-permute-done.9.refs_3_ = f32[160,128]{1,0:T(8,128)S(1)} collective-permute-done((f32[160,128]{1,0:T(8,128)S(1)}, f32[160,128]{1,0:T(8,128)S(1)}, u32[]{:S(2)}, u32[]{:S(2)}) %collective-permute-start.9) | collective-permute-done | bytes 81952 | tf_op jit(solution)/shard_map/ppermute | solution.py:34
  34.0 2.9 %collective-permute-done.8.refs_2_ = f32[160,128]{1,0:T(8,128)S(1)} collective-permute-done((f32[160,128]{1,0:T(8,128)S(1)}, f32[160,128]{1,0:T(8,128)S(1)}, u32[]{:S(2)}, u32[]{:S(2)}) %collective-permute-start.8) | collective-permute-done | bytes 81952 | tf_op jit(solution)/shard_map/ppermute | solution.py:34
  37.0 0.9 %smooth.1 = f32[640,128]{1,0:T(8,128)} custom-call(f32[32,96]{1,0:T(8,128)S(1)} %smoothing_weights.1.weights, f32[160,128]{1,0:T(8,128)S(1)} %pad_maximum_fusion.refs_0_, f32[160,128]{1,0:T(8,128)S(1)} %collective-permute-done.7.refs_1_, f32[160,128]{1,0:T(8,128)S(1)} %collective-permute-done.8.refs_2_, f32[160,128]{1,0:T(8,128)S(1)} %collective-permute-done.9.refs_3_), custom_call_target="tpu_custom_call" | custom-call | tf_op jit(solution)/shard_map/smooth/pallas_call | solution.py:211
  (25 shorter events, 0.2 us)
Async XLA Ops:
  0.0 8.0 %copy-start.1 = (bf16[1,5,128,12]{2,3,1,0:T(8,128)(2,1)S(1)}, bf16[1,5,128,12]{2,3,1,0:T(8,128)(2,1)}, u32[]{:S(2)}) copy-start(bf16[1,5,128,12]{2,3,1,0:T(8,128)(2,1)} %param.9) | copy-start | bytes 46084
  0.0 8.0 %copy-start.2 = (bf16[1,5,16,12]{3,2,1,0:T(8,128)(2,1)S(1)}, bf16[1,5,16,12]{3,2,1,0:T(8,128)(2,1)}, u32[]{:S(2)}) copy-start(bf16[1,5,16,12]{3,2,1,0:T(8,128)(2,1)} %refs_4_.3) | copy-start | bytes 5764
  0.0 8.0 %copy-start.5 = (s32[1,5]{1,0:T(1,128)S(1)}, s32[1,5]{1,0:T(1,128)}, u32[]{:S(2)}) copy-start(s32[1,5]{1,0:T(1,128)} %refs_1_.3) | copy-start | bytes 64
  0.0 8.0 %copy-start.6 = (s32[1,5]{1,0:T(1,128)S(1)}, s32[1,5]{1,0:T(1,128)}, u32[]{:S(2)}) copy-start(s32[1,5]{1,0:T(1,128)} %refs_2_.3) | copy-start | bytes 64
  0.0 8.0 %copy-start.4 = (s32[1,5]{1,0:T(1,128)S(1)}, s32[1,5]{1,0:T(1,128)}, u32[]{:S(2)}) copy-start(s32[1,5]{1,0:T(1,128)} %refs_0_.3) | copy-start | bytes 64
  0.0 8.0 %copy-start = (bf16[4,10,80,512]{3,2,1,0:T(8,128)(2,1)S(1)}, bf16[4,10,80,512]{3,2,1,0:T(8,128)(2,1)}, u32[]{:S(2)}) copy-start(bf16[4,10,80,512]{3,2,1,0:T(8,128)(2,1)} %refs_5_.3) | copy-start | bytes 9830404
  4.7 21.4 %copy-start.3 = (f32[32,32]{1,0:T(8,128)S(1)}, f32[32,32]{1,0:T(8,128)}, u32[]{:S(2)}) copy-start(f32[32,32]{1,0:T(8,128)} %smoother.1) | copy-start | bytes 12292
  4.7 21.4 %copy-start.7 = (s32[32,1]{0,1:T(1,128)S(1)}, s32[32,1]{0,1:T(1,128)}, u32[]{:S(2)}) copy-start(s32[32,1]{0,1:T(1,128)} %param.14) | copy-start | bytes 388
  4.8 9.8 %collective-permute-start = (f32[640,128]{1,0:T(8,128)}, f32[640,128]{1,0:T(8,128)S(1)}, u32[]{:S(2)}, u32[]{:S(2)}) collective-permute-start(f32[640,128]{1,0:T(8,128)} %get-tuple-element.12), channel_id=1, source_target_pairs={{0,1},{1,0},{2,3},{3,2},{4,5},{5,4},{6,7},{7,6},{8,9},{9,8},{10,11... | collective-permute-start | bytes 983048 | tf_op jit(solution)/shard_map/ppermute | solution.py:22
  6.3 12.7 %collective-permute-start.2 = (f32[640,128]{1,0:T(8,128)}, f32[640,128]{1,0:T(8,128)S(1)}, u32[]{:S(2)}, u32[]{:S(2)}) collective-permute-start(f32[640,128]{1,0:T(8,128)} %get-tuple-element.14), channel_id=1, source_target_pairs={{0,32},{1,2},{2,1},{3,4},{4,3},{5,6},{6,5},{7,8},{8,7},{9,10},{10,... | collective-permute-start | bytes 983048 | tf_op jit(solution)/shard_map/ppermute | solution.py:22
  14.5 8.7 %collective-permute-start.1 = (f32[320,128]{1,0:T(8,128)S(1)}, f32[320,128]{1,0:T(8,128)S(1)}, u32[]{:S(2)}, u32[]{:S(2)}) collective-permute-start(f32[320,128]{1,0:T(8,128)S(1)} %get-tuple-element.15), channel_id=1, source_target_pairs={{0,32},{1,2},{2,1},{3,4},{4,3},{5,6},{6,5},{7,8},{8,7},{9,10},{10,... | collective-permute-start | bytes 491528 | tf_op jit(solution)/shard_map/ppermute | solution.py:22
  19.1 6.9 %collective-permute-start.3 = (f32[320,128]{1,0:T(8,128)S(1)}, f32[320,128]{1,0:T(8,128)S(1)}, u32[]{:S(2)}, u32[]{:S(2)}) collective-permute-start(f32[320,128]{1,0:T(8,128)S(1)} %get-tuple-element.17), channel_id=1, source_target_pairs={{0,1},{1,0},{2,3},{3,2},{4,5},{5,4},{6,7},{7,6},{8,9},{9,8},{10,11... | collective-permute-start | bytes 491528 | tf_op jit(solution)/shard_map/ppermute | solution.py:22
  19.2 8.7 %collective-permute-start.5 = (f32[320,128]{1,0:T(8,128)S(1)}, f32[320,128]{1,0:T(8,128)S(1)}, u32[]{:S(2)}, u32[]{:S(2)}) collective-permute-start(f32[320,128]{1,0:T(8,128)S(1)} %get-tuple-element.16), channel_id=1, source_target_pairs={{0,32},{1,34},{2,33},{3,36},{4,35},{5,38},{6,37},{7,40},{8,39},{9,... | collective-permute-start | bytes 491528 | tf_op jit(solution)/shard_map/ppermute | solution.py:22
  19.3 8.6 %collective-permute-start.6 = (f32[320,128]{1,0:T(8,128)S(1)}, f32[320,128]{1,0:T(8,128)S(1)}, u32[]{:S(2)}, u32[]{:S(2)}) collective-permute-start(f32[320,128]{1,0:T(8,128)S(1)} %get-tuple-element.18), channel_id=1, source_target_pairs={{0,33},{1,32},{2,35},{3,34},{4,37},{5,36},{6,39},{7,38},{8,41},{9,... | collective-permute-start | bytes 491528 | tf_op jit(solution)/shard_map/ppermute | solution.py:22
  26.0 1.9 %collective-permute-start.4 = (f32[320,128]{1,0:T(8,128)S(1)}, f32[320,128]{1,0:T(8,128)S(1)}, u32[]{:S(2)}, u32[]{:S(2)}) collective-permute-start(f32[320,128]{1,0:T(8,128)S(1)} %get-tuple-element.20), channel_id=1, source_target_pairs={{0,32},{32,0},{64,96},{96,64},{128,160},{160,128},{192,224},{224,1... | collective-permute-start | bytes 491528 | tf_op jit(solution)/shard_map/ppermute | solution.py:34
  28.0 6.0 %collective-permute-start.9 = (f32[160,128]{1,0:T(8,128)S(1)}, f32[160,128]{1,0:T(8,128)S(1)}, u32[]{:S(2)}, u32[]{:S(2)}) collective-permute-start(f32[160,128]{1,0:T(8,128)S(1)} %pad_maximum_fusion.3), channel_id=1, source_target_pairs={{0,128},{32,160},{64,192},{96,224},{128,0},{160,32},{192,64},{224,... | collective-permute-start | bytes 245768 | tf_op jit(solution)/shard_map/ppermute | solution.py:34
  31.3 5.7 %collective-permute-start.8 = (f32[160,128]{1,0:T(8,128)S(1)}, f32[160,128]{1,0:T(8,128)S(1)}, u32[]{:S(2)}, u32[]{:S(2)}) collective-permute-start(f32[160,128]{1,0:T(8,128)S(1)} %pad_maximum_fusion.2), channel_id=1, source_target_pairs={{0,192},{32,224},{64,128},{96,160},{128,64},{160,96},{192,0},{224,... | collective-permute-start | bytes 245768 | tf_op jit(solution)/shard_map/ppermute | solution.py:34
  32.3 4.6 %collective-permute-start.7 = (f32[160,128]{1,0:T(8,128)S(1)}, f32[160,128]{1,0:T(8,128)S(1)}, u32[]{:S(2)}, u32[]{:S(2)}) collective-permute-start(f32[160,128]{1,0:T(8,128)S(1)} %pad_maximum_fusion.1), channel_id=1, source_target_pairs={{0,64},{32,96},{64,0},{96,32},{128,192},{160,224},{192,128},{224,1... | collective-permute-start | bytes 245768 | tf_op jit(solution)/shard_map/ppermute | solution.py:34

commit v6 on v5

--- a/solution.py
+++ b/solution.py
@@ -113,8 +113,10 @@
             rows = jnp.concatenate([part[n * tile_rows : (n + 1) * tile_rows] for part in along_y], 0)
             high = rows.astype(jnp.bfloat16)
             low = (rows - high.astype(jnp.float32)).astype(jnp.bfloat16)
-            partial = jnp.dot(high, x_mats[n], preferred_element_type=jnp.float32) + jnp.dot(
-                low, x_mats[n], preferred_element_type=jnp.float32
+            partial = jnp.dot(
+                jnp.concatenate([high, low], 1),
+                jnp.concatenate([x_mats[n], x_mats[n]], 0),
+                preferred_element_type=jnp.float32,
             )
             stride = 2 * dates * bands
             for b in range(bands):

time: 38 us -> 37.9 us (level)
  transfers between devices with their start and end apart: 10 -> 10, of which waited for: 7 -> 7; matrix products, arithmetic and copies ran while one was open for 0% -> 0% of each run, Pallas kernels for 10% -> 9%
where the time goes in v6:
time: 37.9 us; the launch traced here: 37.8 us
  waiting for transfers between devices  16 us (42%)
  starting transfers between devices  12.2 us (32%)
  Pallas kernels  9.14 us (24%)
    ppermute x6, waiting for transfers between devices, joint_swap(): return lax.ppermute(block, ('date', 'tile'), pairs)  11.5 us
    pallas_call x2, Pallas kernels, resample(): pl.pallas_call(functools.partial(resample_kernel, reaches), in_specs=[pl....  7.93 us
    ppermute x6, starting transfers between devices, joint_swap(): return lax.ppermute(block, ('date', 'tile'), pairs)  7.75 us
    ppermute x4, waiting for transfers between devices, date_swap(): lax.ppermute(block, 'date', [(i, i ^ distance) for i in range(lax.axis_si...  4.54 us
    ppermute x4, starting transfers between devices, date_swap(): lax.ppermute(block, 'date', [(i, i ^ distance) for i in range(lax.axis_si...  4.46 us
    pallas_call x1, Pallas kernels, smooth(): pl.pallas_call(smooth_kernel, out_shape=jax.ShapeDtypeStruct((sum((piece....  0.93 us
  transfers between devices with their start and end apart: 10, of which 7 were waited for; matrix products, arithmetic and copies ran while one was open for 0% of the time, Pallas kernels for 9%

profile of v6, /device:TPU:128, one launch (start us, length us, event | category | flops | bytes accessed | tf_op | source)
XLA Modules:
  0.0 37.8 jit_solution(17928010794614815206)
XLA Ops:
  0.0 4.6 %resample.3 = (f32[640,128]{1,0:T(8,128)}, f32[640,128]{1,0:T(8,128)}) custom-call(s32[1,5]{1,0:T(1,128)} %refs_0_.3, s32[1,5]{1,0:T(1,128)} %refs_1_.3, s32[1,5]{1,0:T(1,128)} %refs_2_.3, bf16[1,5,12,128]{3,2,1,0:T(8,128)(2,1)} %bitcast.21, bf16[1,5,16,12]{3,2,1,0:T(8,128)(2,1)} %refs_4_.3, bf16[4,10,80,512]{3,2,1,0:T(8,128)(2,1)} %refs_5_.3), custom_call_target="tpu_custom_call" | custom-call | flops 387973120 | bytes 3276800 | tf_op jit(solution)/shard_map/resample/pallas_call | solution.py:134
  4.7 0.0 copy-start.3
  4.7 0.0 copy-start.7
  4.7 1.6 %collective-permute-start = (f32[640,128]{1,0:T(8,128)}, f32[640,128]{1,0:T(8,128)S(1)}, u32[]{:S(2)}, u32[]{:S(2)}) collective-permute-start(f32[640,128]{1,0:T(8,128)} %get-tuple-element.12), channel_id=1, source_target_pairs={{0,1},{1,0},{2,3},{3,2},{4,5},{5,4},{6,7},{7,6},{8,9},{9,8},{10,11... | collective-permute-start | bytes 983048 | tf_op jit(solution)/shard_map/ppermute | solution.py:22
  6.3 1.6 %collective-permute-start.2 = (f32[640,128]{1,0:T(8,128)}, f32[640,128]{1,0:T(8,128)S(1)}, u32[]{:S(2)}, u32[]{:S(2)}) collective-permute-start(f32[640,128]{1,0:T(8,128)} %get-tuple-element.14), channel_id=1, source_target_pairs={{0,32},{1,2},{2,1},{3,4},{4,3},{5,6},{6,5},{7,8},{8,7},{9,10},{10,... | collective-permute-start | bytes 983048 | tf_op jit(solution)/shard_map/ppermute | solution.py:22
  8.0 3.3 %resample.2 = (f32[640,128]{1,0:T(8,128)S(1)}, f32[640,128]{1,0:T(8,128)S(1)}, f32[640,128]{1,0:T(8,128)S(1)}) custom-call(s32[1,5]{1,0:T(1,128)S(1)} %copy-done.4, s32[1,5]{1,0:T(1,128)S(1)} %copy-done.5, s32[1,5]{1,0:T(1,128)S(1)} %copy-done.6, bf16[1,5,12,128]{3,2,1,0:T(8,128)(2,1)S(1)} %bitcast.22, bf16[1,5,16,12]{3,2,1,0:T(8,128)(2,1)S(1)} %copy-done.2, ...), custom_call_target="tpu_custom_call" | custom-call | flops 581959680 | bytes 3276800 | tf_op jit(solution)/shard_map/resample/pallas_call | solution.py:134
  11.3 3.2 %collective-permute-done = f32[640,128]{1,0:T(8,128)S(1)} collective-permute-done((f32[640,128]{1,0:T(8,128)}, f32[640,128]{1,0:T(8,128)S(1)}, u32[]{:S(2)}, u32[]{:S(2)}) %collective-permute-start) | collective-permute-done | bytes 327712 | tf_op jit(solution)/shard_map/ppermute | solution.py:22
  14.5 2.4 %collective-permute-start.1 = (f32[320,128]{1,0:T(8,128)S(1)}, f32[320,128]{1,0:T(8,128)S(1)}, u32[]{:S(2)}, u32[]{:S(2)}) collective-permute-start(f32[320,128]{1,0:T(8,128)S(1)} %get-tuple-element.15), channel_id=1, source_target_pairs={{0,32},{1,2},{2,1},{3,4},{4,3},{5,6},{6,5},{7,8},{8,7},{9,10},{10,... | collective-permute-start | bytes 491528 | tf_op jit(solution)/shard_map/ppermute | solution.py:22
  16.9 2.1 %collective-permute-done.2 = f32[640,128]{1,0:T(8,128)S(1)} collective-permute-done((f32[640,128]{1,0:T(8,128)}, f32[640,128]{1,0:T(8,128)S(1)}, u32[]{:S(2)}, u32[]{:S(2)}) %collective-permute-start.2) | collective-permute-done | bytes 327712 | tf_op jit(solution)/shard_map/ppermute | solution.py:22
  19.0 0.1 collective-permute-start.3
  19.1 0.1 collective-permute-start.5
  19.2 1.9 %collective-permute-start.6 = (f32[320,128]{1,0:T(8,128)S(1)}, f32[320,128]{1,0:T(8,128)S(1)}, u32[]{:S(2)}, u32[]{:S(2)}) collective-permute-start(f32[320,128]{1,0:T(8,128)S(1)} %get-tuple-element.18), channel_id=1, source_target_pairs={{0,33},{1,32},{2,35},{3,34},{4,37},{5,36},{6,39},{7,38},{8,41},{9,... | collective-permute-start | bytes 491528 | tf_op jit(solution)/shard_map/ppermute | solution.py:22
  21.2 2.0 %collective-permute-done.1 = f32[320,128]{1,0:T(8,128)S(1)} collective-permute-done((f32[320,128]{1,0:T(8,128)S(1)}, f32[320,128]{1,0:T(8,128)S(1)}, u32[]{:S(2)}, u32[]{:S(2)}) %collective-permute-start.1) | collective-permute-done | bytes 163872 | tf_op jit(solution)/shard_map/ppermute | solution.py:22
  23.2 2.7 %collective-permute-done.3 = f32[320,128]{1,0:T(8,128)S(1)} collective-permute-done((f32[320,128]{1,0:T(8,128)S(1)}, f32[320,128]{1,0:T(8,128)S(1)}, u32[]{:S(2)}, u32[]{:S(2)}) %collective-permute-start.3) | collective-permute-done | bytes 163872 | tf_op jit(solution)/shard_map/ppermute | solution.py:22
  25.9 0.1 collective-permute-start.4
  26.1 0.3 smoothing_weights.1.weights
  26.4 1.5 %collective-permute-done.5 = f32[320,128]{1,0:T(8,128)S(1)} collective-permute-done((f32[320,128]{1,0:T(8,128)S(1)}, f32[320,128]{1,0:T(8,128)S(1)}, u32[]{:S(2)}, u32[]{:S(2)}) %collective-permute-start.5) | collective-permute-done | bytes 163872 | tf_op jit(solution)/shard_map/ppermute | solution.py:22
  27.8 0.0 collective-permute-done.6
  27.9 3.3 %collective-permute-start.9 = (f32[160,128]{1,0:T(8,128)S(1)}, f32[160,128]{1,0:T(8,128)S(1)}, u32[]{:S(2)}, u32[]{:S(2)}) collective-permute-start(f32[160,128]{1,0:T(8,128)S(1)} %pad_maximum_fusion.3), channel_id=1, source_target_pairs={{0,128},{32,160},{64,192},{96,224},{128,0},{160,32},{192,64},{224,... | collective-permute-start | bytes 245768 | tf_op jit(solution)/shard_map/ppermute | solution.py:34
  31.2 1.1 %collective-permute-start.8 = (f32[160,128]{1,0:T(8,128)S(1)}, f32[160,128]{1,0:T(8,128)S(1)}, u32[]{:S(2)}, u32[]{:S(2)}) collective-permute-start(f32[160,128]{1,0:T(8,128)S(1)} %pad_maximum_fusion.2), channel_id=1, source_target_pairs={{0,192},{32,224},{64,128},{96,160},{128,64},{160,96},{192,0},{224,... | collective-permute-start | bytes 245768 | tf_op jit(solution)/shard_map/ppermute | solution.py:34
  32.3 1.6 %collective-permute-done.9.refs_3_ = f32[160,128]{1,0:T(8,128)S(1)} collective-permute-done((f32[160,128]{1,0:T(8,128)S(1)}, f32[160,128]{1,0:T(8,128)S(1)}, u32[]{:S(2)}, u32[]{:S(2)}) %collective-permute-start.9) | collective-permute-done | bytes 81952 | tf_op jit(solution)/shard_map/ppermute | solution.py:34
  34.0 2.9 %collective-permute-done.8.refs_2_ = f32[160,128]{1,0:T(8,128)S(1)} collective-permute-done((f32[160,128]{1,0:T(8,128)S(1)}, f32[160,128]{1,0:T(8,128)S(1)}, u32[]{:S(2)}, u32[]{:S(2)}) %collective-permute-start.8) | collective-permute-done | bytes 81952 | tf_op jit(solution)/shard_map/ppermute | solution.py:34
  36.9 0.0 collective-permute-done.7.refs_1_
  36.9 0.9 %smooth.1 = f32[640,128]{1,0:T(8,128)} custom-call(f32[32,96]{1,0:T(8,128)S(1)} %smoothing_weights.1.weights, f32[160,128]{1,0:T(8,128)S(1)} %pad_maximum_fusion.refs_0_, f32[160,128]{1,0:T(8,128)S(1)} %collective-permute-done.7.refs_1_, f32[160,128]{1,0:T(8,128)S(1)} %collective-permute-done.8.refs_2_, f32[160,128]{1,0:T(8,128)S(1)} %collective-permute-done.9.refs_3_), custom_call_target="tpu_custom_call" | custom-call | tf_op jit(solution)/shard_map/smooth/pallas_call | solution.py:213
  (25 shorter events, 0.2 us)
Async XLA Ops:
  0.0 7.9 %copy-start.1 = (bf16[1,5,128,12]{2,3,1,0:T(8,128)(2,1)S(1)}, bf16[1,5,128,12]{2,3,1,0:T(8,128)(2,1)}, u32[]{:S(2)}) copy-start(bf16[1,5,128,12]{2,3,1,0:T(8,128)(2,1)} %param.9) | copy-start | bytes 46084
  0.0 7.9 %copy-start.2 = (bf16[1,5,16,12]{3,2,1,0:T(8,128)(2,1)S(1)}, bf16[1,5,16,12]{3,2,1,0:T(8,128)(2,1)}, u32[]{:S(2)}) copy-start(bf16[1,5,16,12]{3,2,1,0:T(8,128)(2,1)} %refs_4_.3) | copy-start | bytes 5764
  0.0 7.9 %copy-start.5 = (s32[1,5]{1,0:T(1,128)S(1)}, s32[1,5]{1,0:T(1,128)}, u32[]{:S(2)}) copy-start(s32[1,5]{1,0:T(1,128)} %refs_1_.3) | copy-start | bytes 64
  0.0 7.9 %copy-start.6 = (s32[1,5]{1,0:T(1,128)S(1)}, s32[1,5]{1,0:T(1,128)}, u32[]{:S(2)}) copy-start(s32[1,5]{1,0:T(1,128)} %refs_2_.3) | copy-start | bytes 64
  0.0 7.9 %copy-start.4 = (s32[1,5]{1,0:T(1,128)S(1)}, s32[1,5]{1,0:T(1,128)}, u32[]{:S(2)}) copy-start(s32[1,5]{1,0:T(1,128)} %refs_0_.3) | copy-start | bytes 64
  0.0 7.9 %copy-start = (bf16[4,10,80,512]{3,2,1,0:T(8,128)(2,1)S(1)}, bf16[4,10,80,512]{3,2,1,0:T(8,128)(2,1)}, u32[]{:S(2)}) copy-start(bf16[4,10,80,512]{3,2,1,0:T(8,128)(2,1)} %refs_5_.3) | copy-start | bytes 9830404
  4.7 21.4 %copy-start.3 = (f32[32,32]{1,0:T(8,128)S(1)}, f32[32,32]{1,0:T(8,128)}, u32[]{:S(2)}) copy-start(f32[32,32]{1,0:T(8,128)} %smoother.1) | copy-start | bytes 12292
  4.7 21.4 %copy-start.7 = (s32[32,1]{0,1:T(1,128)S(1)}, s32[32,1]{0,1:T(1,128)}, u32[]{:S(2)}) copy-start(s32[32,1]{0,1:T(1,128)} %param.14) | copy-start | bytes 388
  4.7 9.7 %collective-permute-start = (f32[640,128]{1,0:T(8,128)}, f32[640,128]{1,0:T(8,128)S(1)}, u32[]{:S(2)}, u32[]{:S(2)}) collective-permute-start(f32[640,128]{1,0:T(8,128)} %get-tuple-element.12), channel_id=1, source_target_pairs={{0,1},{1,0},{2,3},{3,2},{4,5},{5,4},{6,7},{7,6},{8,9},{9,8},{10,11... | collective-permute-start | bytes 983048 | tf_op jit(solution)/shard_map/ppermute | solution.py:22
  6.3 12.7 %collective-permute-start.2 = (f32[640,128]{1,0:T(8,128)}, f32[640,128]{1,0:T(8,128)S(1)}, u32[]{:S(2)}, u32[]{:S(2)}) collective-permute-start(f32[640,128]{1,0:T(8,128)} %get-tuple-element.14), channel_id=1, source_target_pairs={{0,32},{1,2},{2,1},{3,4},{4,3},{5,6},{6,5},{7,8},{8,7},{9,10},{10,... | collective-permute-start | bytes 983048 | tf_op jit(solution)/shard_map/ppermute | solution.py:22
  14.5 8.7 %collective-permute-start.1 = (f32[320,128]{1,0:T(8,128)S(1)}, f32[320,128]{1,0:T(8,128)S(1)}, u32[]{:S(2)}, u32[]{:S(2)}) collective-permute-start(f32[320,128]{1,0:T(8,128)S(1)} %get-tuple-element.15), channel_id=1, source_target_pairs={{0,32},{1,2},{2,1},{3,4},{4,3},{5,6},{6,5},{7,8},{8,7},{9,10},{10,... | collective-permute-start | bytes 491528 | tf_op jit(solution)/shard_map/ppermute | solution.py:22
  19.0 6.9 %collective-permute-start.3 = (f32[320,128]{1,0:T(8,128)S(1)}, f32[320,128]{1,0:T(8,128)S(1)}, u32[]{:S(2)}, u32[]{:S(2)}) collective-permute-start(f32[320,128]{1,0:T(8,128)S(1)} %get-tuple-element.17), channel_id=1, source_target_pairs={{0,1},{1,0},{2,3},{3,2},{4,5},{5,4},{6,7},{7,6},{8,9},{9,8},{10,11... | collective-permute-start | bytes 491528 | tf_op jit(solution)/shard_map/ppermute | solution.py:22
  19.1 8.7 %collective-permute-start.5 = (f32[320,128]{1,0:T(8,128)S(1)}, f32[320,128]{1,0:T(8,128)S(1)}, u32[]{:S(2)}, u32[]{:S(2)}) collective-permute-start(f32[320,128]{1,0:T(8,128)S(1)} %get-tuple-element.16), channel_id=1, source_target_pairs={{0,32},{1,34},{2,33},{3,36},{4,35},{5,38},{6,37},{7,40},{8,39},{9,... | collective-permute-start | bytes 491528 | tf_op jit(solution)/shard_map/ppermute | solution.py:22
  19.2 8.6 %collective-permute-start.6 = (f32[320,128]{1,0:T(8,128)S(1)}, f32[320,128]{1,0:T(8,128)S(1)}, u32[]{:S(2)}, u32[]{:S(2)}) collective-permute-start(f32[320,128]{1,0:T(8,128)S(1)} %get-tuple-element.18), channel_id=1, source_target_pairs={{0,33},{1,32},{2,35},{3,34},{4,37},{5,36},{6,39},{7,38},{8,41},{9,... | collective-permute-start | bytes 491528 | tf_op jit(solution)/shard_map/ppermute | solution.py:22
  25.9 1.9 %collective-permute-start.4 = (f32[320,128]{1,0:T(8,128)S(1)}, f32[320,128]{1,0:T(8,128)S(1)}, u32[]{:S(2)}, u32[]{:S(2)}) collective-permute-start(f32[320,128]{1,0:T(8,128)S(1)} %get-tuple-element.20), channel_id=1, source_target_pairs={{0,32},{32,0},{64,96},{96,64},{128,160},{160,128},{192,224},{224,1... | collective-permute-start | bytes 491528 | tf_op jit(solution)/shard_map/ppermute | solution.py:34
  27.9 6.0 %collective-permute-start.9 = (f32[160,128]{1,0:T(8,128)S(1)}, f32[160,128]{1,0:T(8,128)S(1)}, u32[]{:S(2)}, u32[]{:S(2)}) collective-permute-start(f32[160,128]{1,0:T(8,128)S(1)} %pad_maximum_fusion.3), channel_id=1, source_target_pairs={{0,128},{32,160},{64,192},{96,224},{128,0},{160,32},{192,64},{224,... | collective-permute-start | bytes 245768 | tf_op jit(solution)/shard_map/ppermute | solution.py:34
  31.2 5.7 %collective-permute-start.8 = (f32[160,128]{1,0:T(8,128)S(1)}, f32[160,128]{1,0:T(8,128)S(1)}, u32[]{:S(2)}, u32[]{:S(2)}) collective-permute-start(f32[160,128]{1,0:T(8,128)S(1)} %pad_maximum_fusion.2), channel_id=1, source_target_pairs={{0,192},{32,224},{64,128},{96,160},{128,64},{160,96},{192,0},{224,... | collective-permute-start | bytes 245768 | tf_op jit(solution)/shard_map/ppermute | solution.py:34
  32.3 4.6 %collective-permute-start.7 = (f32[160,128]{1,0:T(8,128)S(1)}, f32[160,128]{1,0:T(8,128)S(1)}, u32[]{:S(2)}, u32[]{:S(2)}) collective-permute-start(f32[160,128]{1,0:T(8,128)S(1)} %pad_maximum_fusion.1), channel_id=1, source_target_pairs={{0,64},{32,96},{64,0},{96,32},{128,192},{160,224},{192,128},{224,1... | collective-permute-start | bytes 245768 | tf_op jit(solution)/shard_map/ppermute | solution.py:34
